TPU v7x, 32 devices: a whole 2x2x4 slice. The times are simulated.
32 devices in a mesh: dp: 8 (over y, x, core), rows: 4 (over z).
Axes of the slice: x: 2, y: 2, z: 4, core: 2. Of those that a mesh axis runs over, the one named last changes fastest.
Arguments:
- inputs: float32 [64, 8, 44, 512], P('rows', 'dp'), may hold values from -60 to 60
- image_ids: int32 [64, 8, 44], P('rows', 'dp'), may hold values from -1 to 6, as said below
- first_norm_gain: float32 [512], replicated, may hold values from 0.5 to 1.5
- first_norm_bias: float32 [512], replicated, may hold values from -0.5 to 0.5
- point_one: float32 [512, 512], replicated, may hold values from -0.25 to 0.25
- kernel_big: float32 [27, 27, 512], replicated, may hold values from -0.21875 to 0.21875
- kernel_small: float32 [5, 5, 512], replicated, may hold values from -1.25 to 1.25
- second_norm_gain: float32 [512], replicated, may hold values from 0.5 to 1.5
- second_norm_bias: float32 [512], replicated, may hold values from -0.5 to 0.5
- point_two: float32 [512, 512], replicated, may hold values from -0.25 to 0.25
- feedforward_norm_gain: float32 [512], replicated, may hold values from 0.5 to 1.5
- feedforward_norm_bias: float32 [512], replicated, may hold values from -0.5 to 0.5
- w_up: float32 [512, 2048], P(None, 'rows'), may hold values from -0.25 to 0.25
- w_down: float32 [2048, 512], P('rows'), may hold values from -0.125 to 0.125
- out_grad: float32 [64, 8, 44, 512], P('rows', 'dp'), may hold values from -6 to 6
Outputs:
- output: float32 [64, 8, 44, 512], P('rows', 'dp')
- grad_input: float32 [64, 8, 44, 512], P('rows', 'dp')
- grad_gain_one: float32 [512], replicated
- grad_bias_one: float32 [512], replicated
- grad_point_one: float32 [512, 512], replicated
- grad_kernel_big: float32 [27, 27, 512], replicated
- grad_kernel_small: float32 [5, 5, 512], replicated
- grad_gain_two: float32 [512], replicated
- grad_bias_two: float32 [512], replicated
- grad_point_two: float32 [512, 512], replicated
- grad_gain_three: float32 [512], replicated
- grad_bias_three: float32 [512], replicated
- grad_w_up: float32 [512, 2048], P(None, 'rows')
- grad_w_down: float32 [2048, 512], P('rows')
Inputs may be any that keep to these rules, and one draw needn't show every extreme that they name: `image_ids`: each canvas packs three square maps of sides 24, 24 and 14 stacked in its left columns and four 14 x 14 maps stacked to their right; ids 0 to 2 name the first three, 3 to 6 the others; -1 marks unused pixels.
All inputs are finite; a program needn't handle non-finite values.
Results may differ from a plain program's by a relative error of at most 0.0003.
Values sent between devices are 32-bit elements; how exact they have to be, the bound alone decides.
A program may use at most 192 MiB of HBM per device.

v0:
```python
import functools

import jax
import jax.numpy as jnp
import numpy as np
from jax import lax
from jax.experimental import pallas as pl
from jax.experimental.pallas import tpu as pltpu
from jax.sharding import PartitionSpec as P

EPSILON = 1e-05
HIGHEST = lax.Precision.HIGHEST
HIGH = lax.Precision.HIGH
MESH = pl.DeviceIdType.MESH
F32 = jnp.float32
BF16 = jnp.bfloat16

LEFT, RIGHT = 24, 16
SLOTS = LEFT + RIGHT
LEFT_IDS = 3
LEFT_N, RIGHT_N = 37, 27
LEFT_F, RIGHT_F = 24, 16
FREQ = 2 * LEFT_F + 2 * RIGHT_F
REACH = 13
SPAN = 2 * REACH + 1
SPAN_PAD = 32
LANES = 128


def forward_transform(length, padded, positions, columns):
    count = length // 2 + 1
    out = np.zeros((2 * padded, columns))
    angle = 2 * np.pi * np.outer(np.arange(count), positions) / length
    out[:count, : len(positions)] = np.cos(angle)
    out[padded : padded + count, : len(positions)] = -np.sin(angle)
    return out


def backward_transform(length, padded, positions, rows):
    count = length // 2 + 1
    out = np.zeros((rows, 2 * padded))
    twice = np.where(np.arange(count) == 0, 1.0, 2.0)
    angle = 2 * np.pi * np.outer(positions, np.arange(count)) / length
    out[: len(positions), :count] = np.cos(angle) * twice / length
    out[: len(positions), padded : padded + count] = -np.sin(angle) * twice / length
    return out


def slots_to_freq():
    out = np.zeros((FREQ, SLOTS))
    out[: 2 * LEFT_F, :LEFT] = forward_transform(LEFT_N, LEFT_F, np.arange(LEFT), LEFT)
    out[2 * LEFT_F :, LEFT:] = forward_transform(RIGHT_N, RIGHT_F, np.arange(RIGHT), RIGHT)
    return out


def freq_to_slots():
    out = np.zeros((SLOTS, FREQ))
    out[:LEFT, : 2 * LEFT_F] = backward_transform(LEFT_N, LEFT_F, np.arange(LEFT), LEFT)
    out[LEFT:, 2 * LEFT_F :] = backward_transform(RIGHT_N, RIGHT_F, np.arange(RIGHT), RIGHT)
    return out


def taps_to_freq():
    taps = np.arange(SPAN) - REACH
    return np.concatenate(
        [
            forward_transform(LEFT_N, LEFT_F, taps, SPAN_PAD),
            forward_transform(RIGHT_N, RIGHT_F, taps, SPAN_PAD),
        ]
    )


def freq_to_taps():
    taps = np.arange(SPAN) - REACH
    return np.concatenate(
        [
            backward_transform(LEFT_N, LEFT_F, taps, SPAN_PAD),
            backward_transform(RIGHT_N, RIGHT_F, taps, SPAN_PAD),
        ],
        axis=1,
    )


def split_constant(matrix, group):
    whole = np.kron(np.eye(group), matrix).astype(np.float32)
    high = whole.astype(jnp.bfloat16)
    low = (whole - high.astype(np.float32)).astype(jnp.bfloat16)
    return np.concatenate([high, high, low], axis=1)


def split_stack(value):
    high = value.astype(BF16)
    low = (value - high.astype(F32)).astype(BF16)
    return jnp.concatenate([high, low, high], axis=0)


def product_split(constant_ref, value):
    return jnp.dot(constant_ref[...], split_stack(value), preferred_element_type=F32)


GROUP_IN = 6
GROUP_OUT = 4
GROUP_TAP = 7
GROUP_GRAD = 4


def transform_window(window, to_freq_ref, out_ref):
    for first in range(0, window.shape[0], GROUP_IN):
        part = window[first : first + GROUP_IN].reshape(GROUP_IN * SLOTS, window.shape[-1])
        freq = product_split(to_freq_ref, part)
        out_ref[first : first + GROUP_IN] = freq.reshape(GROUP_IN, FREQ, freq.shape[-1])


def sum_rows(bounds, rows, x_ref, k_ref, y_ref, flipped, conjugate):
    width = x_ref.shape[-1]
    for side, (start, size) in enumerate(((0, LEFT_F), (2 * LEFT_F, RIGHT_F))):
        real, imag = pl.ds(start, size), pl.ds(start + size, size)

        def one_row(row, carry):
            def tap(w, total):
                index = row + SPAN - 1 - w if flipped else w - row
                xr, xi = x_ref[w, real, :], x_ref[w, imag, :]
                kr, ki = k_ref[index, real, :], k_ref[index, imag, :]
                if conjugate:
                    return (total[0] + kr * xr + ki * xi, total[1] + kr * xi - ki * xr)
                return (total[0] + kr * xr - ki * xi, total[1] + kr * xi + ki * xr)

            zero = jnp.zeros((size, width), F32)
            low, high = bounds[2 * side, row], bounds[2 * side + 1, row]
            yr, yi = lax.fori_loop(low, high, tap, (zero, zero))
            y_ref[row, real, :] = yr
            y_ref[row, imag, :] = yi
            return carry

        lax.fori_loop(0, rows, one_row, 0)


def rows_to_slots(rows, y_ref, to_slots_ref, mask_ref, out_ref):
    for first in range(0, rows, GROUP_OUT):
        freq = y_ref[first : first + GROUP_OUT].reshape(GROUP_OUT * FREQ, y_ref.shape[-1])
        cells = product_split(to_slots_ref, freq).reshape(GROUP_OUT, SLOTS, y_ref.shape[-1])
        out_ref[first : first + GROUP_OUT] = cells * mask_ref[first : first + GROUP_OUT]


def conv_forward_kernel(
    bounds, window, taps, mask, to_freq, taps_freq, to_slots, out, xf, kf, stats, yf
):
    rows = out.shape[0]
    transform_window(window, to_freq, xf)
    for first in range(0, kf.shape[0], GROUP_TAP):
        part = taps[first : first + GROUP_TAP].reshape(GROUP_TAP * SPAN_PAD, taps.shape[-1])
        freq = product_split(taps_freq, part)
        kf[first : first + GROUP_TAP] = freq.reshape(GROUP_TAP, FREQ, freq.shape[-1])
    sum_rows(bounds, rows, xf, kf, yf, False, True)
    rows_to_slots(rows, yf, to_slots, mask, out)
    cells = out[...].reshape(rows * SLOTS, out.shape[-1])
    stats[0:1, :] = jnp.sum(cells, axis=0, keepdims=True)
    stats[1:2, :] = jnp.sum(cells * cells, axis=0, keepdims=True)
    stats[2:8, :] = jnp.zeros((6, stats.shape[-1]), F32)


CHUNK = 256
TAP_ROWS = 28


def chunked(leading):
    return pl.BlockSpec(leading + (CHUNK,), lambda c, *_: (0,) * len(leading) + (c,))


def whole(array):
    return pl.BlockSpec(array.shape, lambda c, *_: (0,) * array.ndim)


def conv_forward(bounds, field, taps, mask):
    window, _, channels = field.shape
    rows = window - 2 * REACH
    constants = [
        jnp.asarray(split_constant(slots_to_freq(), GROUP_IN)),
        jnp.asarray(split_constant(taps_to_freq(), GROUP_TAP)),
        jnp.asarray(split_constant(freq_to_slots(), GROUP_OUT)),
    ]
    return pl.pallas_call(
        conv_forward_kernel,
        grid_spec=pltpu.PrefetchScalarGridSpec(
            num_scalar_prefetch=1,
            grid=(channels // CHUNK,),
            in_specs=[
                chunked((window, SLOTS)),
                chunked((TAP_ROWS, SPAN_PAD)),
                pl.BlockSpec((rows, SLOTS, CHUNK), lambda c, *_: (0, 0, 0)),
            ]
            + [whole(c) for c in constants],
            out_specs=[
                chunked((rows, SLOTS)),
                chunked((window, FREQ)),
                chunked((TAP_ROWS, FREQ)),
                chunked((8,)),
            ],
            scratch_shapes=[
                pltpu.VMEM((rows, FREQ, CHUNK), F32),
            ],
        ),
        out_shape=[
            jax.ShapeDtypeStruct((rows, SLOTS, channels), F32),
            jax.ShapeDtypeStruct((window, FREQ, channels), F32),
            jax.ShapeDtypeStruct((TAP_ROWS, FREQ, channels), F32),
            jax.ShapeDtypeStruct((8, channels), F32),
        ],
        compiler_params=pltpu.CompilerParams(vmem_limit_bytes=36 << 20),
        name="conv_forward",
    )(bounds, field, taps, mask, *constants)


def all_sum_job(net, value, out, line_slots, part, layer_slots):
    own = net.own(value, line_slots.at[net.z])
    own.start()
    sent = [net.copy(value, line_slots.at[net.z], net.line(s)) for s in range(1, net.rows)]
    for one in sent:
        one.start()
    yield
    own.wait()
    for one in sent:
        one.wait()
    total = line_slots[0]
    for index in range(1, net.rows):
        total = total + line_slots[index]
    part[...] = total
    own = net.own(part, layer_slots.at[net.dp])
    own.start()
    sent = [net.copy(part, layer_slots.at[net.dp], net.layer(s)) for s in range(1, net.count)]
    for one in sent:
        one.start()
    yield
    own.wait()
    for one in sent:
        one.wait()
    total = layer_slots[0]
    for index in range(1, net.count):
        total = total + layer_slots[index]
    out[...] = total


class Net:
    def __init__(self, dp, rows, send_sem, recv_sem):
        self.count, self.rows = dp, rows
        self.send_sem, self.recv_sem, self.used = send_sem, recv_sem, 0
        self.dp = lax.axis_index("dp")
        self.z = lax.axis_index("rows")
        self.bits = list(range(1, dp.bit_length() - 1))

    def bit(self, index):
        return lax.rem(self.dp // (1 << index), 2)

    def across(self, index):
        return (self.dp + (1 << index) * (1 - 2 * self.bit(index)), self.z)

    def line(self, step):
        return (self.dp, lax.rem(self.z + step, self.rows))

    def layer(self, step):
        return (lax.rem(self.dp + step, self.count), self.z)

    def greet(self):
        barrier = pltpu.get_barrier_semaphore()

        def greet_line(step, carry):
            pl.semaphore_signal(barrier, inc=1, device_id=self.line(step), device_id_type=MESH)
            return carry

        def greet_layer(step, carry):
            pl.semaphore_signal(barrier, inc=1, device_id=self.layer(step), device_id_type=MESH)
            return carry

        lax.fori_loop(1, self.rows, greet_line, 0)
        lax.fori_loop(1, self.count, greet_layer, 0)

    def ready(self):
        pl.semaphore_wait(pltpu.get_barrier_semaphore(), self.rows + self.count - 2)

    def copy(self, src, dst, device):
        made = pltpu.make_async_remote_copy(
            src_ref=src,
            dst_ref=dst,
            send_sem=self.send_sem.at[self.used],
            recv_sem=self.recv_sem.at[self.used],
            device_id=device,
            device_id_type=MESH,
        )
        self.used += 1
        return made

    def reserve(self, number):
        self.used += number
        return self.used - number

    def copy_at(self, index, src, dst, device):
        return pltpu.make_async_remote_copy(
            src_ref=src,
            dst_ref=dst,
            send_sem=self.send_sem.at[index],
            recv_sem=self.recv_sem.at[index],
            device_id=device,
            device_id_type=MESH,
        )

    def own(self, src, dst):
        made = pltpu.make_async_copy(src, dst, self.recv_sem.at[self.used])
        self.used += 1
        return made


def all_sum_job(net, value, out, line_slots, part, layer_slots):
    own = net.own(value, line_slots.at[net.z])
    own.start()
    sent = [net.copy(value, line_slots.at[net.z], net.line(s)) for s in range(1, net.rows)]
    for one in sent:
        one.start()
    yield
    own.wait()
    for one in sent:
        one.wait()
    total = line_slots[0]
    for index in range(1, net.rows):
        total = total + line_slots[index]
    part[...] = total
    own = net.own(part, layer_slots.at[net.dp])
    own.start()
    sent = [net.copy(part, layer_slots.at[net.dp], net.layer(s)) for s in range(1, net.count)]
    for one in sent:
        one.start()
    yield
    own.wait()
    for one in sent:
        one.wait()
    total = layer_slots[0]
    for index in range(1, net.count):
        total = total + layer_slots[index]
    out[...] = total


def aligned(value, unit):
    return pl.multiple_of(value, unit)


def halving(net, order, rows):
    base, steps = 0, []
    for bit in order:
        steps.append((bit, base, rows))
        rows //= 2
        base = base + net.bit(bit) * rows
    return steps, base, rows


def add_rows(dst, src, count, step):
    def one(i, carry):
        at = aligned(i * step, step)
        to, of = dst(at), src(at)
        to[...] = to[...] + of[...]
        return carry

    lax.fori_loop(0, count // step, one, 0)


def run(*jobs):
    jobs = list(jobs)
    while jobs:
        jobs = [job for job in jobs if next(job, StopIteration) is not StopIteration]


def line_gather_job(net, value, out):
    own = net.own(value, out.at[net.z])
    own.start()
    sent = [net.copy(value, out.at[net.z], net.line(s)) for s in range(1, net.rows)]
    for one in sent:
        one.start()
    yield
    own.wait()
    for one in sent:
        one.wait()


def sides(net, rows):
    core = net.bit(0)
    return [
        (pl.ds(aligned((2 * core + side) * LANES, LANES), LANES), *halving(net, order, rows))
        for side, order in enumerate((net.bits, net.bits[::-1]))
    ]


def weights_line_job(net, up, down, wall):
    own = [net.own(up, wall.at[net.z, 0]), net.own(down, wall.at[net.z, 1])]
    last = net.rows - 1
    for step in range(1, net.rows):
        moves = []
        for lanes, _, base, rows in sides(net, up.shape[0]):
            mine = pl.ds(aligned(base, 8), rows)
            for way in (1, -1):
                shard = net.z - way * (step - 1)
                going = (net.z >= step - 1) & (net.z < last) if way > 0 else (net.z <= last - (step - 1)) & (net.z > 0)
                coming = net.z >= step if way > 0 else net.z <= last - step
                shard = lax.rem(shard + net.rows, net.rows)
                for which, ref in enumerate((up, down)):
                    piece = wall.at[shard, which, mine, lanes]
                    one = net.copy(ref.at[mine, lanes] if step == 1 else piece, piece, net.line(way % net.rows))
                    pl.when(going)(one.start)
                    moves.append((one, going, coming))
        if step == 1:
            for one in own:
                one.start()
        yield
        for one, going, coming in moves:
            pl.when(coming)(one.wait_recv)
            pl.when(going)(one.wait_send)
    for one in own:
        one.wait()


def weights_layer_job(net, wall):
    parts = sides(net, wall.shape[2])
    for back in range(1, len(net.bits) + 1):
        moves = []
        for lanes, steps, _, _ in parts:
            bit, base, rows = steps[-back]
            mine = pl.ds(aligned(base + net.bit(bit) * (rows // 2), 8), rows // 2)
            for step in range(1, net.rows):
                piece = wall.at[lax.rem(net.z + step, net.rows), :, mine, lanes]
                moves.append(net.copy(piece, piece, net.across(bit)))
        for one in moves:
            one.start()
        yield
        for one in moves:
            one.wait()


def weights_pair_job(net, wall):
    half = wall.shape[3] // 2
    lanes = pl.ds(aligned(net.bit(0) * half, LANES), half)
    moves = []
    for step in range(1, net.rows):
        piece = wall.at[lax.rem(net.z + step, net.rows), :, :, lanes]
        moves.append(net.copy(piece, piece, net.across(0)))
    for one in moves:
        one.start()
    yield
    for one in moves:
        one.wait()


def halo_job(net, field, window, zeros):
    rows = field.shape[0]
    own = net.own(field, window.at[pl.ds(REACH, rows)])
    own.start()
    has_above, has_below = net.z > 0, net.z < net.rows - 1
    down = net.copy(field.at[pl.ds(rows - REACH, REACH)], window.at[pl.ds(0, REACH)], net.line(1))
    up = net.copy(field.at[pl.ds(0, REACH)], window.at[pl.ds(REACH + rows, REACH)], net.line(net.rows - 1))
    pl.when(has_below)(down.start)
    pl.when(has_above)(up.start)
    zeros[...] = jnp.zeros(zeros.shape, F32)
    top = net.own(zeros, window.at[pl.ds(0, REACH)])
    bottom = net.own(zeros, window.at[pl.ds(REACH + rows, REACH)])
    pl.when(jnp.logical_not(has_above))(top.start)
    pl.when(jnp.logical_not(has_below))(bottom.start)
    yield
    own.wait()
    pl.when(jnp.logical_not(has_above))(top.wait)
    pl.when(jnp.logical_not(has_below))(bottom.wait)
    pl.when(has_above)(down.wait_recv)
    pl.when(has_below)(down.wait_send)
    pl.when(has_below)(up.wait_recv)
    pl.when(has_above)(up.wait_send)


def shares(net, rows, width):
    core, out = net.bit(0), []
    by_rows = width == 2 * LANES
    for side, order in enumerate((net.bits, net.bits[::-1])):
        start = side * (rows // 2) if by_rows else 0
        steps, base, size = halving(net, order, rows // 2 if by_rows else rows)
        steps = [(bit, start + first, count) for bit, first, count in steps]
        block = 0 if by_rows else side
        outer = pl.ds(aligned((core if by_rows else 2 * core + side) * LANES, LANES), LANES)
        out.append((pl.ds(block * LANES, LANES), outer, steps, start + base, size))
    return out


def reduce_all_job(net, source, acc, got_pair, got, got_line, out):
    rows, width = source.shape
    half = width // 2
    core = net.bit(0)
    own = net.own(source.at[:, pl.ds(aligned(core * half, LANES), half)], acc)
    sent = net.copy(source.at[:, pl.ds(aligned((1 - core) * half, LANES), half)], got_pair, net.across(0))
    own.start()
    sent.start()
    yield
    own.wait()
    sent.wait()
    add_rows(lambda at: acc.at[pl.ds(at, 64)], lambda at: got_pair.at[pl.ds(at, 64)], rows, 64)
    parts = shares(net, rows, width)
    for index in range(len(net.bits)):
        moves = []
        for side, (inner, _, steps, _, _) in enumerate(parts):
            bit, base, size = steps[index]
            size //= 2
            give = base + (1 - net.bit(bit)) * size
            keep = base + net.bit(bit) * size
            place = got.at[side, pl.ds(rows - 2 * size, size)]
            one = net.copy(acc.at[pl.ds(aligned(give, 8), size), inner], place, net.across(bit))
            one.start()
            moves.append((one, keep, size, inner, side))
        yield
        for one, keep, size, inner, side in moves:
            one.wait()
            unit = 64 if size % 64 == 0 else 8
            add_rows(
                lambda at: acc.at[pl.ds(aligned(keep + at, 8), unit), inner],
                lambda at: got.at[side, pl.ds(aligned(rows - 2 * size + at, 8), unit)],
                size,
                unit,
            )
    moves, own = [], []
    for side, (inner, _, _, base, size) in enumerate(parts):
        size //= net.rows
        own.append(net.own(acc.at[pl.ds(aligned(base + net.z * size, 8), size), inner], got_line.at[side, net.z]))
        for step in range(1, net.rows):
            other = lax.rem(net.z + step, net.rows)
            piece = acc.at[pl.ds(aligned(base + other * size, 8), size), inner]
            moves.append(net.copy(piece, got_line.at[side, net.z], net.line(step)))
    for one in own + moves:
        one.start()
    yield
    for one in own + moves:
        one.wait()
    moves = []
    for side, (_, outer, _, base, size) in enumerate(parts):
        size //= net.rows
        total = got_line[side, 0]
        for index in range(1, net.rows):
            total = total + got_line[side, index]
        piece = out.at[pl.ds(aligned(base + net.z * size, 8), size), outer]
        out[pl.ds(aligned(base + net.z * size, 8), size), outer] = total
        for step in range(1, net.rows):
            moves.append(net.copy(piece, piece, net.line(step)))
            moves[-1].start()
    yield
    for one in moves:
        one.wait()
    for back in range(1, len(net.bits) + 1):
        moves = []
        for _, outer, steps, _, _ in parts:
            bit, base, size = steps[-back]
            piece = out.at[pl.ds(aligned(base + net.bit(bit) * (size // 2), 8), size // 2), outer]
            moves.append(net.copy(piece, piece, net.across(bit)))
            moves[-1].start()
        yield
        for one in moves:
            one.wait()
    piece = out.at[:, pl.ds(aligned(core * half, LANES), half)]
    one = net.copy(piece, piece, net.across(0))
    one.start()
    yield
    one.wait()


VMEM = pl.BlockSpec(memory_space=pltpu.VMEM)
HBM = pl.BlockSpec(memory_space=pltpu.HBM)
COPIES = 448


def shape(*dims):
    return jax.ShapeDtypeStruct(dims, F32)


def exchange(name, number, mesh, body, args, in_specs, outs, out_specs, scratch, limit, aliases=None, late=False):
    dp, rows = mesh

    def kernel(*refs):
        *refs, send_sem, recv_sem = refs
        net = Net(dp, rows, send_sem, recv_sem)
        net.greet()
        if not late:
            net.ready()
        body(net, *refs)
        assert net.used <= COPIES

    return pl.pallas_call(
        kernel,
        out_shape=outs,
        in_specs=in_specs,
        out_specs=out_specs,
        scratch_shapes=scratch + [pltpu.SemaphoreType.DMA((COPIES,))] * 2,
        input_output_aliases=aliases or {},
        compiler_params=pltpu.CompilerParams(
            collective_id=number, has_side_effects=True, vmem_limit_bytes=limit << 20
        ),
        name=name,
    )(*args)


def sum_scratch(mesh, height):
    dp, rows = mesh
    return [pltpu.VMEM((rows, height, LANES), F32), pltpu.VMEM((height, LANES), F32), pltpu.VMEM((dp, height, LANES), F32)]


def sums_names_weights(mesh, value, names, up, down):
    rows = mesh[1]

    def body(net, value, names, up, down, total, all_names, wall, *slots):
        run(
            weights_line_job(net, up, down, wall),
            line_gather_job(net, names, all_names),
            all_sum_job(net, value, total, *slots),
        )

    return exchange(
        "sums_one",
        0,
        mesh,
        body,
        (value, names, up, down),
        [VMEM] * 4,
        [
            shape(*value.shape),
            jax.ShapeDtypeStruct((rows,) + names.shape, jnp.int32),
            shape(rows, 2, *up.shape),
        ],
        [VMEM, VMEM, HBM],
        sum_scratch(mesh, value.shape[0]),
        16,
    )


def halo_weights(mesh, field, wall):
    rows = field.shape[0]

    def body(net, field, wall_in, window, wall, zeros):
        halo = halo_job(net, field, window, zeros)
        next(halo)
        run(weights_layer_job(net, wall))
        run(weights_pair_job(net, wall))
        finish(halo)

    return exchange(
        "halo_act",
        1,
        mesh,
        body,
        (field, wall),
        [VMEM, HBM],
        [shape(rows + 2 * REACH, *field.shape[1:]), shape(*wall.shape)],
        [HBM, HBM],
        [pltpu.VMEM((REACH,) + field.shape[1:], F32)],
        16,
        {1: 1},
    )


def all_scratch(mesh, rows, width):
    size = (rows // 2 if width == 2 * LANES else rows) * 2 // mesh[0] // mesh[1]
    return [
        pltpu.VMEM((rows, width // 2), F32),
        pltpu.VMEM((rows, width // 2), F32),
        pltpu.VMEM((2, rows, LANES), F32),
        pltpu.VMEM((2, mesh[1], size, LANES), F32),
    ]


class Loads:
    def __init__(self, sems):
        self.sems, self.used, self.leaving = sems, 0, []

    def start(self, src, dst):
        one = pltpu.make_async_copy(src, dst, self.sems.at[self.used])
        self.used += 1
        one.start()
        return one

    def leave(self, src, dst):
        self.leaving.append(self.start(src, dst))

    def finish(self):
        for one in self.leaving:
            one.wait()


def gelu_parts(x):
    scale, cubic = 0.7978845608028654, 0.044715
    square = x * x
    t = jnp.tanh(scale * (x + cubic * (x * square)))
    half = 0.5 * (1.0 + t)
    return (x * half, half + 0.5 * x * (1.0 - t * t) * (scale * (1.0 + 3.0 * cubic * square)))


NN = (((1,), (0,)), ((), ()))
NT = (((1,), (1,)), ((), ()))
TILE = 320


def split_two(value):
    high = value.astype(BF16)
    return high, (value - high.astype(F32)).astype(BF16)


def store_split(refs, where, value):
    refs[0][where], refs[1][where] = split_two(value)


def dot_split(left, right, dims=NN):
    def one(a, b):
        return lax.dot_general(a, b, dims, preferred_element_type=F32)

    return one(left[0], right[0]) + (one(left[0], right[1]) + one(left[1], right[0]))


def read_pair(refs, where=Ellipsis):
    return refs[0][where], refs[1][where]


def write_sums(value, first, second):
    for row in range(4):
        lanes = slice(row * LANES, (row + 1) * LANES)
        value[row : row + 1, :] = first[:, lanes]
        value[4 + row : 5 + row, :] = second[:, lanes]


def read_sums(total):
    return tuple(
        jnp.concatenate([total[4 * k + row : 4 * k + row + 1, :] for row in range(4)], axis=1) for k in range(2)
    )


def column_sum(value):
    return jnp.sum(value, axis=0, keepdims=True)


def norm_terms(total, count):
    first, second = read_sums(total)
    mean = first / count
    return mean, lax.rsqrt(second / count - mean * mean + EPSILON)


def finish(job):
    for _ in job:
        pass


def rem(value, unit):
    return value % unit if isinstance(value, int) else lax.rem(value, unit)


def middle_kernel(
    net,
    conv,
    conv_sums,
    x,
    gy,
    mask,
    params,
    point_two,
    wall,
    delta,
    back,
    total_four,
    total_five,
    dconv,
    point_grad,
    part,
    sums_own,
    sums_slots,
    own_sem,
    mixed,
    xhat,
    slope_two,
    act_pair,
    u_pair,
    ut_pair,
    g_pair,
    gt_pair,
    point_pair,
    up_pair,
    down_pair,
    hid_pair,
    dpre_pair,
    w_up,
    w_down,
    made,
    acc,
    got_pair,
    got_layer,
    got_line,
):
    pixels, channels = conv.shape
    tiles = pixels // TILE
    hidden = w_up.shape[2]
    per_shard = wall.shape[2] // hidden
    chunks = net.rows * per_shard
    core = net.bit(0)
    gain_two, bias_two, gain_three, bias_three, count = (params[row : row + 1, :] for row in range(5))

    def each_tile(body):
        def one(index, carry):
            return body(pl.ds(aligned(index * TILE, TILE), TILE), carry)

        zero = jnp.zeros((1, channels), F32)
        return lax.fori_loop(0, tiles, one, (zero, zero))

    def valid(rows):
        return jnp.concatenate([mask[rows, :]] * (channels // LANES), axis=1)

    def total_job(which, out):
        return all_sum_job(net, sums_own.at[which], out, *(slots.at[which] for slots in sums_slots))

    def shard_of(chunk):
        return lax.rem(net.z + chunk // per_shard, net.rows)

    def load(chunk):
        slot, shard, part = rem(chunk, 2), shard_of(chunk), rem(chunk, per_shard)
        span = pl.ds(aligned(part * hidden, hidden), hidden)
        return (
            pltpu.make_async_copy(wall.at[shard, 0, :, span], w_up.at[slot], own_sem.at[0, slot]),
            pltpu.make_async_copy(wall.at[shard, 1, span, :], w_down.at[slot], own_sem.at[1, slot]),
        )

    sums_own[0] = conv_sums[...]
    net.ready()
    job = total_job(0, sums_slots[1].at[0])
    next(job)
    for one in load(0):
        one.start()
    store_split(point_pair, Ellipsis, point_two[...])
    store_split(g_pair, Ellipsis, gy[...])
    next(job)
    store_split(gt_pair, Ellipsis, gy[...].T)
    finish(job)
    mean, inv_two = norm_terms(sums_slots[1].at[0], count)

    def second_norm(rows, carry):
        m = valid(rows)
        hat = (conv[rows, :] - mean) * inv_two
        act, slope = gelu_parts((hat * gain_two + bias_two) * m)
        xhat[rows, :] = hat
        slope_two[rows, :] = slope * m
        store_split(act_pair, rows, act)
        field = x[rows, :] + dot_split(read_pair(act_pair, rows), read_pair(point_pair))
        mixed[rows, :] = field
        return carry[0] + column_sum(field), carry[1] + column_sum(field * field)

    write_sums(sums_own.at[1], *each_tile(second_norm))
    job = total_job(1, sums_slots[1].at[1])
    next(job)
    next(job)
    finish(job)
    mean_three, inv_three = norm_terms(sums_slots[1].at[1], count)

    def third_norm(rows, carry):
        hat = (mixed[rows, :] - mean_three) * inv_three
        store_split(u_pair, rows, (hat * gain_three + bias_three) * valid(rows))
        delta[rows, :] = mixed[rows, :] - x[rows, :]
        back[rows, :] = jnp.zeros((TILE, channels), F32)
        return carry

    each_tile(third_norm)
    for side in range(2):
        ut_pair[side][...] = u_pair[side][...].T

    mine = pl.ds(aligned(core * LANES, LANES), LANES)
    other = pl.ds(aligned((1 - core) * LANES, LANES), LANES)
    halvings = [halving(net, order, channels) for order in (net.bits, net.bits[::-1])]
    stages = len(net.bits)
    pair_base = net.reserve(chunks)
    layer_base = net.reserve(2 * stages * chunks)
    line_base = net.reserve(2 * chunks)

    def pair_move(chunk):
        slot = rem(chunk, 2)
        return (
            net.copy_at(pair_base + chunk, made.at[slot, :, :, other], got_pair.at[chunk], net.across(0)),
            pltpu.make_async_copy(made.at[slot, :, :, mine], acc.at[chunk], own_sem.at[2, slot]),
        )

    def layer_move(stage, chunk):
        moves = []
        for side, (steps, _, _) in enumerate(halvings):
            bit, base, size = steps[stage]
            size //= 2
            give, keep = base + (1 - net.bit(bit)) * size, base + net.bit(bit) * size
            place = pl.ds(channels - 2 * size, size)
            moves.append(
                (
                    net.copy_at(
                        layer_base + (2 * stage + side) * chunks + chunk,
                        acc.at[chunk, side, pl.ds(aligned(give, 8), size), :],
                        got_layer.at[chunk, side, place, :],
                        net.across(bit),
                    ),
                    keep,
                    size,
                    side,
                )
            )
        return moves

    def line_move(chunk, remote):
        moves = []
        shard, part = shard_of(chunk), rem(chunk, per_shard)
        for side, (_, base, size) in enumerate(halvings):
            piece = acc.at[chunk, side, pl.ds(aligned(base, 8), size), :]
            place = got_line.at[net.z, part, side]
            if remote:
                moves.append(net.copy_at(line_base + 2 * chunk + side, piece, place, (net.dp, shard)))
            else:
                moves.append(pltpu.make_async_copy(piece, place, net.recv_sem.at[line_base + 2 * chunk + side]))
        return moves

    def when(test, body):
        if isinstance(test, bool):
            if test:
                body()
        else:
            pl.when(test)(body)

    def within(chunk):
        if isinstance(chunk, int):
            return 0 <= chunk < chunks
        return (chunk >= 0) & (chunk < chunks)

    def progress(step):
        def after_pair():
            chunk = step - 1
            sent, own = pair_move(chunk)
            own.wait()
            sent.wait()
            for side in range(2):
                add_rows(
                    lambda at: acc.at[chunk, side, pl.ds(at, 64), :],
                    lambda at: got_pair.at[chunk, side, pl.ds(at, 64), :],
                    channels,
                    64,
                )
            for one, *_ in layer_move(0, chunk):
                one.start()

        def after_layer(stage):
            chunk = step - 2 - stage
            for one, keep, size, side in layer_move(stage, chunk):
                one.wait()
                unit = min(size, 64)
                add_rows(
                    lambda at: acc.at[chunk, side, pl.ds(aligned(keep + at, 8), unit), :],
                    lambda at: got_layer.at[chunk, side, pl.ds(aligned(channels - 2 * size + at, 8), unit), :],
                    size,
                    unit,
                )
            if stage + 1 < stages:
                for one, *_ in layer_move(stage + 1, chunk):
                    one.start()
            else:

                def go(remote):
                    def start():
                        for one in line_move(chunk, remote):
                            one.start()

                    return start

                when(chunk >= per_shard, go(True))
                when(chunk < per_shard, go(False))

        when(within(step - 1), after_pair)
        for stage in range(stages):
            when(within(step - 2 - stage), functools.partial(after_layer, stage))

    def feed_forward(chunk, carry):
        progress(chunk)
        slot = rem(chunk, 2)
        for one in load(chunk):
            one.wait()

        @pl.when(chunk + 1 < chunks)
        def _():
            for one in load(chunk + 1):
                one.start()

        store_split(up_pair, Ellipsis, w_up[slot])
        store_split(down_pair, Ellipsis, w_down[slot])

        def first_half(rows, carry):
            hid, slope = gelu_parts(dot_split(read_pair(u_pair, rows), read_pair(up_pair)))
            store_split(hid_pair, rows, hid)
            store_split(
                dpre_pair, rows, dot_split(read_pair(g_pair, rows), read_pair(down_pair), NT) * slope
            )
            return carry

        each_tile(first_half)
        made[slot, 0] = dot_split(read_pair(ut_pair), read_pair(dpre_pair))
        made[slot, 1] = dot_split(read_pair(gt_pair), read_pair(hid_pair))
        for one in pair_move(chunk):
            one.start()

        def second_half(rows, carry):
            delta[rows, :] += dot_split(read_pair(hid_pair, rows), read_pair(down_pair))
            back[rows, :] += dot_split(read_pair(dpre_pair, rows), read_pair(up_pair), NT)
            return carry

        each_tile(second_half)
        return carry

    lax.fori_loop(0, chunks, feed_forward, 0)

    def third_sums(rows, carry):
        dy = back[rows, :] * valid(rows)
        back[rows, :] = dy
        hat = (mixed[rows, :] - mean_three) * inv_three
        return carry[0] + column_sum(dy), carry[1] + column_sum(dy * hat)

    write_sums(sums_own.at[2], *each_tile(third_sums))
    job = total_job(2, total_four)
    next(job)
    progress(chunks)
    next(job)
    progress(chunks + 1)
    finish(job)
    for step in range(chunks + 2, chunks + 1 + stages):
        progress(step)
    grad_bias, grad_gain = read_sums(total_four)

    def third_back(rows, carry):
        m = valid(rows)
        hat = (mixed[rows, :] - mean_three) * inv_three
        field = m * gain_three * inv_three * (back[rows, :] - grad_bias / count - hat * (grad_gain / count))
        back[rows, :] = field
        dmixed = gy[rows, :] + field
        store_split(g_pair, rows, dmixed)
        du = dot_split(read_pair(g_pair, rows), read_pair(point_pair), NT) * slope_two[rows, :]
        mixed[rows, :] = du
        return carry[0] + column_sum(du), carry[1] + column_sum(du * xhat[rows, :])

    write_sums(sums_own.at[3], *each_tile(third_back))
    job = total_job(3, total_five)
    next(job)
    for side in range(2):
        ut_pair[side][...] = act_pair[side][...].T
    next(job)
    point_grad[...] = dot_split(read_pair(ut_pair), read_pair(g_pair))
    finish(job)
    grad_bias_two, grad_gain_two = read_sums(total_five)

    def second_back(row, carry):
        rows = pl.ds(aligned(row * SLOTS, 8), SLOTS)
        field = mixed[rows, :] - grad_bias_two / count - xhat[rows, :] * (grad_gain_two / count)
        dconv[row] = valid(rows) * gain_two * inv_two * field
        return carry

    lax.fori_loop(0, pixels // SLOTS, second_back, 0)
    for chunk in range(chunks):
        for one in line_move(chunk, chunk >= per_shard):
            one.wait()
    for which in range(2):
        for block in range(per_shard):
            total = got_line[0, block, which]
            for index in range(1, net.rows):
                total = total + got_line[index, block, which]
            part[which, block] = total


def middle(mesh, conv, conv_sums, x, gy, mask, params, point_two, wall):
    dp, rows = mesh
    pixels, channels = conv.shape
    hidden = 2 * LANES
    chunks = rows * (wall.shape[2] // hidden)
    lines = pixels // SLOTS

    def pair(*dims):
        return [pltpu.VMEM(dims, BF16)] * 2

    piece = channels * 2 // dp
    scratch = [
        pltpu.VMEM((4, 8, LANES), F32),
        [pltpu.VMEM((4, rows, 8, LANES), F32), pltpu.VMEM((4, 8, LANES), F32), pltpu.VMEM((4, dp, 8, LANES), F32)],
        pltpu.SemaphoreType.DMA((3, 2)),
        pltpu.VMEM((pixels, channels), F32),
        pltpu.VMEM((pixels, channels), F32),
        pltpu.VMEM((pixels, channels), F32),
        pair(pixels, channels),
        pair(pixels, channels),
        pair(channels, pixels),
        pair(pixels, channels),
        pair(channels, pixels),
        pair(channels, channels),
        pair(channels, hidden),
        pair(hidden, channels),
        pair(pixels, hidden),
        pair(pixels, hidden),
        pltpu.VMEM((2, channels, hidden), F32),
        pltpu.VMEM((2, hidden, channels), F32),
        pltpu.VMEM((2, 2, channels, hidden), F32),
        pltpu.VMEM((chunks, 2, channels, LANES), F32),
        pltpu.VMEM((chunks, 2, channels, LANES), F32),
        pltpu.VMEM((chunks, 2, channels, LANES), F32),
        pltpu.VMEM((rows, wall.shape[2] // hidden, 2, piece, LANES), F32),
    ]
    return exchange(
        "middle",
        2,
        mesh,
        middle_kernel,
        (conv, conv_sums, x, gy, mask, params, point_two, wall),
        [VMEM] * 7 + [HBM],
        [shape(pixels, channels)] * 2
        + [shape(8, LANES)] * 2
        + [shape(lines, SLOTS, channels), shape(channels, channels)]
        + [shape(2, wall.shape[2] // hidden, piece, LANES)],
        [VMEM] * 7,
        scratch,
        56,
        late=True,
    )


ZERO_ROW = 42
WINDOW_PAD = 48
LEFT_TAPS, RIGHT_TAPS = 24, 14
SIDES = ((0, LEFT_F, LEFT_TAPS), (2 * LEFT_F, RIGHT_F, RIGHT_TAPS))


def transform(window, to_freq, out, group):
    rows, _, width = window.shape
    for first in range(0, rows, group):
        part = window[first : first + group].reshape(group * SLOTS, width)
        out[first : first + group] = product_split(to_freq, part).reshape(group, FREQ, width)


def sum_table(table, rows, x_ref, k_ref, y_ref, flipped):
    width = x_ref.shape[-1]
    for side, (start, size, taps) in enumerate(SIDES):
        real, imag = pl.ds(start, size), pl.ds(start + size, size)

        def one_row(row, carry):
            yr, yi = jnp.zeros((size, width), F32), jnp.zeros((size, width), F32)
            for tap in range(taps):
                w = table[side * rows + row, tap]
                index = jnp.clip(row + SPAN - 1 - w if flipped else w - row, 0, SPAN)
                xr, xi = x_ref[w, real, :], x_ref[w, imag, :]
                kr, ki = k_ref[index, real, :], k_ref[index, imag, :]
                if flipped:
                    yr, yi = yr + (kr * xr - ki * xi), yi + (kr * xi + ki * xr)
                else:
                    yr, yi = yr + (kr * xr + ki * xi), yi + (kr * xi - ki * xr)
            y_ref[row, real, :] = yr
            y_ref[row, imag, :] = yi
            return carry

        lax.fori_loop(0, rows, one_row, 0)


TAP_GROUP = 9


def sum_taps(table, rows, d_ref, x_ref, g_ref):
    tile = (8, x_ref.shape[-1])
    for side, (start, size, _) in enumerate(SIDES):
        for first in range(start, start + size, 8):
            real, imag = pl.ds(first, 8), pl.ds(first + size, 8)

            def some_taps(group, carry):
                sums = [(jnp.zeros(tile, F32), jnp.zeros(tile, F32)) for _ in range(TAP_GROUP)]
                for row in range(rows):
                    dr, di = d_ref[REACH + row, real, :], d_ref[REACH + row, imag, :]
                    for k in range(TAP_GROUP):
                        w = table[side * SPAN + group * TAP_GROUP + k, row]
                        xr, xi = x_ref[w, real, :], x_ref[w, imag, :]
                        gr, gi = sums[k]
                        sums[k] = gr + (dr * xr + di * xi), gi + (dr * xi - di * xr)
                for k in range(TAP_GROUP):
                    g_ref[group * TAP_GROUP + k, real, :], g_ref[group * TAP_GROUP + k, imag, :] = sums[k]
                return carry

            lax.fori_loop(0, SPAN // TAP_GROUP, some_taps, 0)


def halo_moves(net, field, window, index):
    rows = field.shape[0]
    lanes = pl.ds(index * LANES, LANES)
    below, above = net.z < net.rows - 1, net.z > 0
    down = net.copy(
        field.at[pl.ds(rows - REACH, REACH), :, lanes], window.at[index, pl.ds(0, REACH)], net.line(1)
    )
    up = net.copy(
        field.at[pl.ds(0, REACH), :, lanes], window.at[index, pl.ds(REACH + rows, REACH)], net.line(net.rows - 1)
    )
    return [(down, below, above), (up, above, below)]


def start_halo(net, field, window):
    rows = field.shape[0]
    moves = [halo_moves(net, field, window, index) for index in range(window.shape[0])]
    for block in moves:
        for one, goes, _ in block:
            pl.when(goes)(one.start)
    empty = jnp.zeros((REACH,) + window.shape[2:], F32)
    for index in range(window.shape[0]):
        window[index, REACH : REACH + rows] = field[:, :, index * LANES : (index + 1) * LANES]
        window[index, 2 * REACH + rows :] = jnp.zeros(
            (window.shape[1] - 2 * REACH - rows,) + window.shape[2:], F32
        )

        @pl.when(net.z == 0)
        def _():
            window[index, :REACH] = empty

        @pl.when(net.z == net.rows - 1)
        def _():
            window[index, REACH + rows : 2 * REACH + rows] = empty

    def wait(index):
        for one, goes, comes in moves[index]:
            pl.when(comes)(one.wait_recv)
            pl.when(goes)(one.wait_send)

    return wait


def last_kernel(
    net,
    row_table,
    tap_table,
    dconv_in,
    xf,
    kf,
    mask_in,
    x_in,
    h_in,
    point_in,
    params,
    back_in,
    part_in,
    point_grad_in,
    to_freq,
    to_slots,
    to_taps,
    cells_out,
    total,
    one_out,
    two_out,
    up_out,
    down_out,
    cube_out,
    dconv,
    mask,
    xhat,
    slope,
    point_one,
    back_three,
    part,
    point_grad,
    load_sem,
    sums_own,
    sums_slots,
    own_sem,
    window,
    df,
    x_block,
    k_block,
    gf,
    yf,
    taps,
    taps_flat,
    cube,
    ut_pair,
    point_pair,
    dh_pair,
    du,
    one_grad,
    grad_one,
    grad_two,
    grad_up,
    down_t,
    two_scratch,
    one_scratch,
    taps_scratch,
):
    rows, _, channels = dconv.shape
    pixels = rows * SLOTS
    blocks = channels // LANES
    gain, inv, count, mean, bias = (params[row : row + 1, :] for row in range(5))
    loads = Loads(load_sem)
    came_dconv = loads.start(dconv_in, dconv)
    came_grad = loads.start(point_grad_in, point_grad)
    came_part = loads.start(part_in, part)
    came_x = loads.start(x_in, xhat)
    came_h = loads.start(h_in, slope)
    came_mask = loads.start(mask_in, mask)
    came_point = loads.start(point_in, point_one)

    def load_x(index):
        return pltpu.make_async_copy(
            xf.at[:, :, pl.ds(index * LANES, LANES)], x_block[index % 2].at[pl.ds(0, xf.shape[0])], own_sem.at[index % 2]
        )

    def load_k(index):
        return pltpu.make_async_copy(
            kf.at[:, :, pl.ds(index * LANES, LANES)], k_block[index % 2], own_sem.at[2 + index % 2]
        )

    load_k(0).start()
    load_x(0).start()
    came_back = loads.start(back_in, back_three)
    came_dconv.wait()
    net.ready()
    wait_halo = start_halo(net, dconv, window)
    came_grad.wait()
    came_part.wait()

    def keep_weights():
        point_one[...] = down_t[...].T
        loads.leave(point_one, down_out)
        loads.leave(grad_up, up_out)

    def keep_taps(half):
        lanes = pl.ds(half * 2 * LANES, 2 * LANES)
        for row in range(SPAN):
            cube[row, :, lanes] = taps_flat[half][row * SPAN : (row + 1) * SPAN, :]
        loads.leave(cube.at[:, :, lanes], cube_out.at[:, :, lanes])

    def then(job, after):
        yield from job
        after()

    background = [
        then(reduce_all_job(net, point_grad, *two_scratch, grad_two), lambda: loads.leave(grad_two, two_out)),
        then(gather_pieces_job(net, part, (grad_up, down_t)), keep_weights),
    ]

    def progress():
        background[:] = [job for job in background if next(job, StopIteration) is not StopIteration]

    progress()
    came_x.wait()
    came_h.wait()
    came_mask.wait()
    came_point.wait()

    def valid(where):
        return jnp.concatenate([mask[where, :]] * blocks, axis=1)

    def prepare(index, carry):
        where = pl.ds(aligned(index * LANES, LANES), LANES)
        hat = (xhat[where, :] - mean) * inv
        xhat[where, :] = hat
        m = valid(where)
        for side, half in enumerate(split_two(((hat * gain + bias) * m).T)):
            ut_pair[side][:, where] = half
        slope[where, :] = gelu_parts(slope[where, :])[1] * m
        return carry

    lax.fori_loop(0, pixels // LANES, prepare, 0)
    store_split(point_pair, Ellipsis, point_one[...])
    for slot in range(2):
        x_block[slot][ZERO_ROW:] = jnp.zeros((1,) + x_block[slot].shape[1:], F32)
    taps[:, SPAN * SPAN :, :] = jnp.zeros((taps.shape[0], taps.shape[1] - SPAN * SPAN, taps.shape[2]), F32)

    for index in range(blocks):
        load_k(index).wait()
        if index + 1 < blocks:
            load_k(index + 1).start()
        wait_halo(index)
        lanes = slice(index * LANES, (index + 1) * LANES)
        transform(window.at[index], to_freq, df.at[index], to_freq.shape[0] // FREQ)
        sum_table(row_table, rows, df.at[index], k_block[index % 2], yf, True)
        group = to_slots.shape[0] // SLOTS
        for first in range(0, rows, group):
            where = slice(first * SLOTS, (first + group) * SLOTS)
            dact = product_split(to_slots, yf[first : first + group].reshape(group * FREQ, LANES))
            dh_pair[0][where, lanes], dh_pair[1][where, lanes] = split_two(dact * slope[where, lanes])
    progress()
    one_grad[...] = dot_split(read_pair(ut_pair), read_pair(dh_pair))
    background.append(then(reduce_all_job(net, one_grad, *one_scratch, grad_one), lambda: loads.leave(grad_one, one_out)))
    progress()

    def last_sums(index, carry):
        where = pl.ds(aligned(index * TILE, TILE), TILE)
        dy = dot_split(read_pair(dh_pair, where), read_pair(point_pair), NT) * valid(where)
        du[where, :] = dy
        return carry[0] + column_sum(dy), carry[1] + column_sum(dy * xhat[where, :])

    zero = jnp.zeros((1, channels), F32)
    write_sums(sums_own, *lax.fori_loop(0, pixels // TILE, last_sums, (zero, zero)))
    background.append(all_sum_job(net, sums_own, total, *sums_slots))
    progress()
    for index in range(blocks):
        load_x(index).wait()
        if index + 1 < blocks:
            load_x(index + 1).start()
        sum_taps(tap_table, rows, df.at[index], x_block[index % 2], gf)
        group = to_taps.shape[0] // SPAN_PAD
        half, lanes = index // 2, slice(index % 2 * LANES, (index % 2 + 1) * LANES)
        for first in range(0, SPAN, group):
            out = product_split(to_taps, gf[first : first + group].reshape(group * FREQ, LANES))
            out = out.reshape(group, SPAN_PAD, LANES)
            for row in range(first, first + group):
                taps[half, row * SPAN : (row + 1) * SPAN, lanes] = out[row - first, :SPAN]
        if index % 2:
            job = reduce_all_job(net, taps.at[half], *taps_scratch[half], taps_flat[half])
            background.append(then(job, functools.partial(keep_taps, half)))
        progress()
    grad_bias, grad_gain = read_sums(total)
    came_back.wait()

    def last_back(index, carry):
        where = pl.ds(aligned(index * TILE, TILE), TILE)
        field = du[where, :] - grad_bias / count - xhat[where, :] * (grad_gain / count)
        back_three[where, :] += valid(where) * gain * inv * field
        return carry

    lax.fori_loop(0, pixels // TILE, last_back, 0)
    loads.leave(back_three, cells_out)
    while background:
        progress()
    loads.finish()


def gather_pieces_job(net, part, outs):
    core = net.bit(0)
    _, per_shard, size, _ = part.shape
    rows = outs[0].shape[0]
    halvings = [halving(net, order, rows) for order in (net.bits, net.bits[::-1])]

    def lanes(block):
        return pl.ds(aligned((2 * block + core) * LANES, LANES), LANES)

    own = []
    for which, out in enumerate(outs):
        base = halvings[which][1]
        for block in range(per_shard):
            own.append(net.own(part.at[which, block], out.at[pl.ds(aligned(base, 8), size), lanes(block)]))
            own[-1].start()
    for one in own:
        one.wait()
    for back_step in range(1, len(net.bits) + 1):
        moves = []
        for which, out in enumerate(outs):
            bit, base, span = halvings[which][0][-back_step]
            here = pl.ds(aligned(base + net.bit(bit) * (span // 2), 8), span // 2)
            for block in range(per_shard):
                piece = out.at[here, lanes(block)]
                moves.append(net.copy(piece, piece, net.across(bit)))
                moves[-1].start()
        yield
        for one in moves:
            one.wait()
    moves = []
    for out in outs:
        for block in range(per_shard):
            piece = out.at[:, lanes(block)]
            moves.append(net.copy(piece, piece, net.across(0)))
            moves[-1].start()
    yield
    for one in moves:
        one.wait()


def last(mesh, tables, dconv, xf, kf, mask, x, hidden, point_one, params, back_three, part, point_grad):
    dp, rows = mesh
    lines, _, channels = dconv.shape
    pixels = lines * SLOTS
    blocks = channels // LANES
    unit = 8 * dp * rows
    tap_rows = -(-SPAN * SPAN // unit) * unit
    constants = [
        jnp.asarray(split_constant(slots_to_freq(), 2)),
        jnp.asarray(split_constant(freq_to_slots(), 2)),
        jnp.asarray(split_constant(freq_to_taps(), 3)),
    ]

    def pair(*dims):
        return [pltpu.VMEM(dims, BF16)] * 2

    field = pltpu.VMEM((pixels, channels), F32)
    square = pltpu.VMEM((channels, channels), F32)
    scratch = [
        pltpu.VMEM(dconv.shape, F32),
        pltpu.VMEM(mask.shape, F32),
        field,
        field,
        square,
        field,
        pltpu.VMEM(part.shape, F32),
        square,
        pltpu.SemaphoreType.DMA((16,)),
        pltpu.VMEM((8, LANES), F32),
        sum_scratch(mesh, 8),
        pltpu.SemaphoreType.DMA((4,)),
        pltpu.VMEM((blocks, WINDOW_PAD, SLOTS, LANES), F32),
        pltpu.VMEM((blocks, WINDOW_PAD, FREQ, LANES), F32),
        [pltpu.VMEM((ZERO_ROW + 1, FREQ, LANES), F32)] * 2,
        [pltpu.VMEM((TAP_ROWS, FREQ, LANES), F32)] * 2,
        pltpu.VMEM((SPAN, FREQ, LANES), F32),
        pltpu.VMEM((lines, FREQ, LANES), F32),
        pltpu.VMEM((blocks // 2, tap_rows, 2 * LANES), F32),
        [pltpu.VMEM((tap_rows, 2 * LANES), F32)] * (blocks // 2),
        pltpu.VMEM((SPAN, SPAN, channels), F32),
        pair(channels, pixels),
        pair(channels, channels),
        pair(pixels, channels),
        field,
        square,
        square,
        square,
        square,
        square,
        all_scratch(mesh, channels, channels),
        all_scratch(mesh, channels, channels),
        [all_scratch(mesh, tap_rows, 2 * LANES)] * (blocks // 2),
    ]
    smem = pl.BlockSpec(memory_space=pltpu.SMEM)
    return exchange(
        "last",
        3,
        mesh,
        last_kernel,
        (*tables, dconv, xf, kf, mask, x, hidden, point_one, params, back_three, part, point_grad, *constants),
        [smem] * 2 + [HBM] * 7 + [VMEM] + [HBM] * 3 + [VMEM] * 3,
        [shape(pixels, channels), shape(8, LANES)] + [shape(channels, channels)] * 4 + [shape(SPAN, SPAN, channels)],
        [HBM, VMEM] + [HBM] * 5,
        scratch,
        60,
        late=True,
    )


def product(left, right):
    return jnp.dot(left, right, precision=HIGH, preferred_element_type=F32)


def product_t(left, right):
    return lax.dot_general(left, right, (((1,), (1,)), ((), ())), precision=HIGH, preferred_element_type=F32)


def contract(left, right):
    return lax.dot_general(left, right, (((0,), (0,)), ((), ())), precision=HIGH, preferred_element_type=F32)


def shards(
    dp,
    devices_rows,
    inputs,
    image_ids,
    first_norm_gain,
    first_norm_bias,
    point_one,
    kernel_big,
    kernel_small,
    second_norm_gain,
    second_norm_bias,
    point_two,
    feedforward_norm_gain,
    feedforward_norm_bias,
    w_up,
    w_down,
    out_grad,
):
    rows, canvases, columns, channels = inputs.shape
    assert canvases == 1 and kernel_big.shape[0] == SPAN
    pixels = rows * SLOTS
    ids = image_ids[:, 0]
    mesh = (dp, devices_rows)

    place = jnp.arange(columns, dtype=jnp.int32)[None, :]
    is_left = (ids >= 0) & (ids < LEFT_IDS)
    is_right = ids >= LEFT_IDS

    def side(member, width):
        name = jnp.max(jnp.where(member, ids, -1), axis=1)
        first = jnp.min(jnp.where(member, place, columns), axis=1)
        return name, jnp.minimum(first, columns - width)

    left_id, left_at = side(is_left, LEFT)
    right_id, right_at = side(is_right, RIGHT)
    slot_column = jnp.concatenate(
        [
            left_at[:, None] + jnp.arange(LEFT, dtype=jnp.int32)[None, :],
            right_at[:, None] + jnp.arange(RIGHT, dtype=jnp.int32)[None, :],
        ],
        axis=1,
    )
    slot_id = jnp.concatenate(
        [
            jnp.broadcast_to(left_id[:, None], (rows, LEFT)),
            jnp.broadcast_to(right_id[:, None], (rows, RIGHT)),
        ],
        axis=1,
    )
    hit = (slot_column[:, :, None] == place[:, None, :]) & (ids[:, None, :] == slot_id[:, :, None])
    hit = hit & (slot_id[:, :, None] >= 0)
    pick = hit.astype(F32)
    slot_mask = jnp.max(pick, axis=2)
    valid = (ids >= 0).astype(F32)

    def compact(field):
        out = lax.dot_general(
            pick, field[:, 0], (((2,), (1,)), ((0,), (0,))), precision=HIGHEST, preferred_element_type=F32
        )
        return out.reshape(pixels, channels)

    def expand(cells):
        return lax.dot_general(
            pick,
            cells.reshape(rows, SLOTS, channels),
            (((1,), (1,)), ((0,), (0,))),
            precision=HIGHEST,
            preferred_element_type=F32,
        )[:, None]

    def pack(first, second):
        return jnp.stack([first, second]).reshape(2 * channels // LANES, LANES)

    def sums(field):
        return jnp.sum(field, axis=0), jnp.sum(field * field, axis=0)

    names = jnp.stack([left_id, right_id], axis=1) + 1
    names_tile = jnp.pad(names.reshape(1, 2 * rows), ((0, 7), (0, LANES - 2 * rows)))
    x = compact(inputs)
    gy = compact(out_grad)
    total, all_names, wall = sums_names_weights(
        mesh,
        jnp.concatenate([pack(*sums(x)), pack(jnp.full((channels,), jnp.sum(valid)), jnp.zeros((channels,)))]),
        names_tile,
        w_up,
        w_down,
    )
    count = total[8, 0]
    total = total[:8].reshape(2, channels)
    all_names = jnp.pad(all_names[:, 0, : 2 * rows].reshape(devices_rows * rows, 2), ((REACH, REACH), (0, 0)))
    window_rows = rows + 2 * REACH
    window_names = lax.dynamic_slice_in_dim(all_names, lax.axis_index("rows") * rows, window_rows, 0)
    w_index = jnp.arange(window_rows, dtype=jnp.int32)[None, :]
    r_index = jnp.arange(rows, dtype=jnp.int32)[:, None]
    near = (w_index >= r_index) & (w_index <= r_index + 2 * REACH)
    bounds = []
    for which in range(2):
        same = near & (names[:, which][:, None] == window_names[:, which][None, :]) & (names[:, which][:, None] > 0)
        low = jnp.min(jnp.where(same, w_index, window_rows), axis=1)
        high = jnp.max(jnp.where(same, w_index + 1, 0), axis=1)
        bounds += [jnp.minimum(low, high), high]
    bounds = jnp.stack(bounds).astype(jnp.int32)
    low, high = bounds[0::2][:, :, None], bounds[1::2][:, :, None]
    listed = low + jnp.arange(LEFT_TAPS, dtype=jnp.int32)
    row_table = jnp.where(listed < high, listed, ZERO_ROW).reshape(2 * rows, LEFT_TAPS)
    listed = jnp.arange(rows, dtype=jnp.int32)[:, None] + jnp.arange(SPAN, dtype=jnp.int32)
    listed = jnp.where((listed >= low) & (listed < high), listed, ZERO_ROW)
    tables = (row_table, listed.transpose(0, 2, 1).reshape(2 * SPAN, rows))

    mask = slot_mask.reshape(pixels, 1)
    mask_wide = jnp.broadcast_to(slot_mask[:, :, None], (rows, SLOTS, CHUNK))

    def norm_scale(total):
        mean = total[0] / count
        return mean, lax.rsqrt(total[1] / count - mean * mean + EPSILON)

    mean_one, inv_one = norm_scale(total)
    xhat_one = (x - mean_one) * inv_one
    u1 = (xhat_one * first_norm_gain + first_norm_bias) * mask
    h1 = product(u1, point_one)
    act, act_slope = gelu_parts(h1)
    act = act.reshape(rows, SLOTS, channels)
    small_start = REACH - kernel_small.shape[0] // 2
    edge = (small_start, small_start)
    kernel = kernel_big + jnp.pad(kernel_small, (edge, edge, (0, 0)))
    taps = jnp.pad(kernel, ((0, TAP_ROWS - SPAN), (0, SPAN_PAD - SPAN), (0, 0)))
    act_window, wall = halo_weights(mesh, act, wall)
    conv, xf, kf, conv_sums = conv_forward(bounds, act_window, taps, mask_wide)
    conv = conv.reshape(pixels, channels)
    conv_sums = conv_sums[:2].reshape(8, LANES)
    vectors = [second_norm_gain, second_norm_bias, feedforward_norm_gain, feedforward_norm_bias]
    params = jnp.stack(vectors + [jnp.full((channels,), count)] + [jnp.zeros((channels,), F32)] * 3)
    mask_lanes = jnp.broadcast_to(mask, (pixels, LANES))
    delta, back_three, total_four, total_five, dconv, point_grad, part = middle(
        mesh, conv, conv_sums, x, gy, mask_lanes, params, point_two, wall
    )
    grad_bias_three, grad_gain_three = total_four.reshape(2, channels)
    grad_bias_two, grad_gain_two = total_five.reshape(2, channels)
    params = jnp.stack(
        [first_norm_gain, inv_one, jnp.full((channels,), count), mean_one, first_norm_bias]
        + [jnp.zeros((channels,), F32)] * 3
    )
    cells, total, grad_point_one, grad_point_two, grad_up, grad_down, grad_kernel = last(
        mesh, tables, dconv, xf, kf, mask_lanes, x, h1, point_one, params, back_three, part, point_grad
    )
    grad_bias_one, grad_gain_one = total.reshape(2, channels)
    output = inputs + expand(delta)
    grad_input = out_grad + expand(cells)
    small_end = small_start + kernel_small.shape[0]
    grad_small = grad_kernel[small_start:small_end, small_start:small_end]
    return (
        output,
        grad_input,
        grad_gain_one,
        grad_bias_one,
        grad_point_one,
        grad_kernel,
        grad_small,
        grad_gain_two,
        grad_bias_two,
        grad_point_two,
        grad_gain_three,
        grad_bias_three,
        grad_up,
        grad_down,
    )


def solution(mesh):
    field = P("rows", "dp", None, None)
    everywhere = P()
    up, down = P(None, "rows"), P("rows", None)
    return jax.shard_map(
        functools.partial(shards, mesh.shape["dp"], mesh.shape["rows"]),
        mesh=mesh,
        in_specs=(field, P("rows", "dp", None)) + (everywhere,) * 10 + (up, down, field),
        out_specs=(field, field) + (everywhere,) * 10 + (up, down),
        check_vma=False,
    )
```

profile of v0, /device:TPU:0, one launch (start us, length us, event | category | flops | bytes accessed | tf_op | source)
XLA Modules:
  0.0 356.5 jit_solution(10133380617560992956)
XLA Ops:
  0.6 0.8 select_reduce_fusion.5
  2.0 2.6 fusion.37
  4.7 0.7 convert_reduce_fusion.1
  5.4 0.6 stack.56
  6.6 34.5 %sums_one.1 = (f32[16,128]{1,0:T(8,128)S(1)}, s32[4,8,128]{2,1,0:T(8,128)S(1)}, f32[4,2,512,512]{3,2,1,0:T(8,128)S(1)}) custom-call(f32[16,128]{1,0:T(8,128)S(1)} %pad_maximum_fusion.refs_0_, s32[8,128]{1,0:T(8,128)S(1)} %pad.17.refs_1_, f32[512,512]{1,0:T(8,128)S(1)} %copy-done.5, f32[512,512]{1,0:T(8,128)S(1)} %copy-done.6), custom_call_target="tpu_custom_call" | custom-call | tf_op jit(solution)/shard_map/sums_one/pallas_call | solution.py:585
  41.2 3.2 copy-done
  44.4 0.5 slice.55
  44.9 0.7 fusion.32
  45.5 0.4 convert_reduce_fusion
  46.1 3.9 %fusion.12 = (f32[640,512]{1,0:T(8,128)S(1)}, f32[640,512]{1,0:T(8,128)}) fusion(f32[512,512]{1,0:T(8,128)} %refs_8_.1, f32[640,512]{1,0:T(8,128)S(1)} %bitcast.82, f32[640]{0:T(1024)S(1)} %mul.80, f32[512]{0:T(512)S(1)} %copy-done.27, f32[512]{0:T(512)S(1)} %copy-done.28, f32[512]{0:T(512)S(1)} %get-tuple-element.130, f32[512]{0:T(512)S(1)} %bitcast.95), kind=kOutput, calls=%fused_computation.16 | convolution fusion | flops 1010892800 | bytes 4991488 | tf_op jit(solution)/shard_map/dot_general | solution.py:1532
  50.0 3.4 copy-done.1
  53.3 43.9 %halo_act.1 = (f32[42,40,512]{2,1,0:T(8,128)S(1)}, f32[4,2,512,512]{3,2,1,0:T(8,128)S(1)}) custom-call(f32[16,40,512]{2,1,0:T(8,128)S(1)} %bitcast.81, f32[4,2,512,512]{3,2,1,0:T(8,128)S(1)} %copy-done.1), custom_call_target="tpu_custom_call", output_to_operand_aliasing={{1}: (1, {})} | custom-call | tf_op jit(solution)/shard_map/halo_act/pallas_call | solution.py:585
  97.3 3.2 copy-done.2
  100.6 0.2 fusion.27
  100.8 0.2 select_reduce_fusion.1
  101.2 1.7 pad_add_fusion
  103.0 0.2 pad.20.taps
  103.1 0.9 copy-done.7
  104.1 0.2 copy-done.8
  104.4 19.2 %conv_forward.1 = (f32[16,40,512]{2,1,0:T(8,128)S(1)}, f32[42,80,512]{2,1,0:T(8,128)}, f32[28,80,512]{2,1,0:T(8,128)S(1)}, f32[8,512]{1,0:T(8,128)S(1)}) custom-call(s32[4,16]{1,0:T(4,128)S(1)} %pad_add_fusion.3.bounds, f32[42,40,512]{2,1,0:T(8,128)S(1)} %get-tuple-element.40.window, f32[28,32,512]{2,1,0:T(8,128)S(1)} %pad.20.taps, ...), custom_call_target="tpu_custom_call" | custom-call | tf_op jit(solution)/shard_map/conv_forward/pallas_call | solution.py:182
  123.6 2.1 copy-done.3
  125.7 1.1 copy-done.4
  126.8 0.6 reshape.235.refs_1_
  127.4 0.6 div.50
  128.1 0.6 stack.65.refs_5_
  128.7 0.9 broadcast_in_dim.131.refs_4_.refs_5_
  129.6 3.4 fusion
  133.0 95.9 %middle.1 = (f32[640,512]{1,0:T(8,128)}, f32[640,512]{1,0:T(8,128)}, f32[8,128]{1,0:T(8,128)}, f32[8,128]{1,0:T(8,128)}, f32[16,40,512]{2,1,0:T(8,128)}, /*index=5*/f32[512,512]{1,0:T(8,128)}, f32[2,2,128,128]{3,2,1,0:T(8,128)}) custom-call(f32[640,512]{1,0:T(8,128)} %bitcast.80, f32[8,128]{1,0:T(8,128)} %reshape.235.refs_1_, f32[640,512]{1,0:T(8,128)} %bitcast.83, ...), custom_call_target="tpu_custom_call" | custom-call | tf_op jit(solution)/shard_map/middle/pallas_call | solution.py:585
  228.8 0.6 stack.66.refs_9_
  230.4 0.6 and_select_fusion.refs_1_
  231.2 0.7 compare_select_fusion.refs_0_
  231.9 104.9 %last.1 = (f32[640,512]{1,0:T(8,128)}, f32[8,128]{1,0:T(8,128)}, f32[512,512]{1,0:T(8,128)}, f32[512,512]{1,0:T(8,128)}, f32[512,512]{1,0:T(8,128)}, /*index=5*/f32[512,512]{1,0:T(8,128)}, f32[27,27,512]{2,1,0:T(8,128)}) custom-call(s32[32,24]{1,0:T(8,128)} %compare_select_fusion.refs_0_, s32[54,16]{1,0:T(8,128)} %and_select_fusion.refs_1_, ...), custom_call_target="tpu_custom_call" | custom-call | tf_op jit(solution)/shard_map/last/pallas_call | solution.py:585
  336.8 2.9 bitcast_add_fusion
  339.8 2.6 copy.87
  342.3 0.6 slice.60
  343.0 0.6 slice_bitcast_fusion.4
  343.6 1.7 bitcast_add_fusion.1
  345.3 2.6 copy.86
  347.9 0.6 slice_bitcast_fusion.2
  348.4 0.6 slice_bitcast_fusion
  349.0 1.0 copy.108
  350.0 1.2 copy.109
  351.2 0.7 copy-done.17
  351.9 1.0 copy.110
  352.8 0.6 copy-done.16
  353.5 1.0 copy.111
  354.4 0.6 copy-done.15
  355.1 1.0 copy.112
  (98 shorter events, 2.7 us)
Async XLA Ops:
  2.0 2.7 copy-start.19
  2.0 4.6 %copy-start.5 = (f32[512,512]{1,0:T(8,128)S(1)}, f32[512,512]{1,0:T(8,128)}, u32[]{:S(2)}) copy-start(f32[512,512]{1,0:T(8,128)} %refs_2_.1) | copy-start | bytes 3145732
  2.0 4.6 %copy-start.6 = (f32[512,512]{1,0:T(8,128)S(1)}, f32[512,512]{1,0:T(8,128)}, u32[]{:S(2)}) copy-start(f32[512,512]{1,0:T(8,128)} %refs_3_.1) | copy-start | bytes 3145732
  4.6 45.3 %copy-start.10 = (f32[16,40,512]{2,1,0:T(8,128)}, f32[16,40,512]{2,1,0:T(8,128)S(1)}, u32[]{:S(2)}) copy-start(f32[16,40,512]{2,1,0:T(8,128)S(1)} %get-tuple-element.143) | copy-start | bytes 3932164
  4.6 41.4 %copy-start.27 = (f32[512]{0:T(512)S(1)}, f32[512]{0:T(512)}, u32[]{:S(2)}) copy-start(f32[512]{0:T(512)} %param.24) | copy-start | bytes 6148
  4.7 41.4 %copy-start.28 = (f32[512]{0:T(512)S(1)}, f32[512]{0:T(512)}, u32[]{:S(2)}) copy-start(f32[512]{0:T(512)} %param.23) | copy-start | bytes 6148
  41.2 3.2 copy-start
  50.0 3.4 copy-start.1
  97.3 3.2 copy-start.2
  102.9 1.2 copy-start.7
  102.9 1.4 copy-start.8
  102.9 1.4 copy-start.9
  104.4 23.7 %copy-start.23 = (f32[512]{0:T(512)S(1)}, f32[512]{0:T(512)}, u32[]{:S(2)}) copy-start(f32[512]{0:T(512)} %param.28) | copy-start | bytes 6148
  104.4 23.7 %copy-start.24 = (f32[512]{0:T(512)S(1)}, f32[512]{0:T(512)}, u32[]{:S(2)}) copy-start(f32[512]{0:T(512)} %param.29) | copy-start | bytes 6148
  104.4 23.7 %copy-start.25 = (f32[512]{0:T(512)S(1)}, f32[512]{0:T(512)}, u32[]{:S(2)}) copy-start(f32[512]{0:T(512)} %param.31) | copy-start | bytes 6148
  104.4 23.7 %copy-start.26 = (f32[512]{0:T(512)S(1)}, f32[512]{0:T(512)}, u32[]{:S(2)}) copy-start(f32[512]{0:T(512)} %param.32) | copy-start | bytes 6148
  123.6 2.1 copy-start.3
  125.7 1.1 copy-start.4
  231.9 104.9 %copy-start.11 = (f32[16,1,44,512]{3,1,2,0:T(1,128)S(1)}, f32[16,1,44,512]{3,1,2,0:T(1,128)}, u32[]{:S(2)}) copy-start(f32[16,1,44,512]{3,1,2,0:T(1,128)} %param.35) | copy-start | bytes 4325380
  336.8 5.5 %copy-start.13 = (f32[27,27,512]{2,1,0:T(8,128)S(1)}, f32[27,27,512]{2,1,0:T(8,128)}, u32[]{:S(2)}) copy-start(f32[27,27,512]{2,1,0:T(8,128)} %get-tuple-element.167) | copy-start | bytes 4478980
  339.7 3.3 copy-start.22
  339.7 3.8 %copy-start.12 = (f32[16,1,44,512]{3,1,2,0:T(1,128)S(1)}, f32[16,1,44,512]{3,1,2,0:T(1,128)}, u32[]{:S(2)}) copy-start(f32[16,1,44,512]{3,1,2,0:T(1,128)} %param.21) | copy-start | bytes 4325380
  339.8 3.8 %copy-start.14 = (f32[640,512]{1,0:T(8,128)S(1)}, f32[640,512]{1,0:T(8,128)}, u32[]{:S(2)}) copy-start(f32[640,512]{1,0:T(8,128)} %get-tuple-element.44) | copy-start | bytes 3932164
  345.2 2.6 copy-start.21
  345.3 3.2 copy-start.20
  345.3 3.8 %copy-start.18 = (f32[512,512]{1,0:T(8,128)S(1)}, f32[512,512]{1,0:T(8,128)}, u32[]{:S(2)}) copy-start(f32[512,512]{1,0:T(8,128)} %get-tuple-element.166) | copy-start | bytes 3145732
  350.0 1.9 copy-start.17
  351.9 1.6 copy-start.16
  353.5 1.6 copy-start.15
where the time goes:
time: 363 us; the launch traced here: 356 us
  Pallas kernels  298 us (82%)
  local copies, waits for them, and re-layouts  35.8 us (10%)
  matrix products  14.4 us (4%)
  other arithmetic  6.41 us (2%)
    pallas_call x4, Pallas kernels, exchange(): pl.pallas_call(kernel, out_shape=outs, in_specs=in_specs, out_specs=out_s...  279 us
    unnamed x65, local copies, waits for them, and re-layouts  26.4 us
    pallas_call x1, Pallas kernels, conv_forward(): pl.pallas_call(conv_forward_kernel, grid_spec=pltpu.PrefetchScalarGridSpe...  19.2 us

commit v1 on v0

--- a/solution.py
+++ b/solution.py
@@ -98,117 +98,76 @@
     return jnp.dot(constant_ref[...], split_stack(value), preferred_element_type=F32)
 
 
-GROUP_IN = 6
-GROUP_OUT = 4
-GROUP_TAP = 7
-GROUP_GRAD = 4
-
-
-def transform_window(window, to_freq_ref, out_ref):
-    for first in range(0, window.shape[0], GROUP_IN):
-        part = window[first : first + GROUP_IN].reshape(GROUP_IN * SLOTS, window.shape[-1])
-        freq = product_split(to_freq_ref, part)
-        out_ref[first : first + GROUP_IN] = freq.reshape(GROUP_IN, FREQ, freq.shape[-1])
-
-
-def sum_rows(bounds, rows, x_ref, k_ref, y_ref, flipped, conjugate):
-    width = x_ref.shape[-1]
-    for side, (start, size) in enumerate(((0, LEFT_F), (2 * LEFT_F, RIGHT_F))):
-        real, imag = pl.ds(start, size), pl.ds(start + size, size)
-
-        def one_row(row, carry):
-            def tap(w, total):
-                index = row + SPAN - 1 - w if flipped else w - row
-                xr, xi = x_ref[w, real, :], x_ref[w, imag, :]
-                kr, ki = k_ref[index, real, :], k_ref[index, imag, :]
-                if conjugate:
-                    return (total[0] + kr * xr + ki * xi, total[1] + kr * xi - ki * xr)
-                return (total[0] + kr * xr - ki * xi, total[1] + kr * xi + ki * xr)
-
-            zero = jnp.zeros((size, width), F32)
-            low, high = bounds[2 * side, row], bounds[2 * side + 1, row]
-            yr, yi = lax.fori_loop(low, high, tap, (zero, zero))
-            y_ref[row, real, :] = yr
-            y_ref[row, imag, :] = yi
+TAP_ROWS = 28
+
+
+class Net:
+    def __init__(self, dp, rows, send_sem, recv_sem):
+        self.count, self.rows = dp, rows
+        self.send_sem, self.recv_sem, self.used = send_sem, recv_sem, 0
+        self.dp = lax.axis_index("dp")
+        self.z = lax.axis_index("rows")
+        self.bits = list(range(1, dp.bit_length() - 1))
+
+    def bit(self, index):
+        return lax.rem(self.dp // (1 << index), 2)
+
+    def across(self, index):
+        return (self.dp + (1 << index) * (1 - 2 * self.bit(index)), self.z)
+
+    def line(self, step):
+        return (self.dp, lax.rem(self.z + step, self.rows))
+
+    def layer(self, step):
+        return (lax.rem(self.dp + step, self.count), self.z)
+
+    def greet(self):
+        barrier = pltpu.get_barrier_semaphore()
+
+        def greet_line(step, carry):
+            pl.semaphore_signal(barrier, inc=1, device_id=self.line(step), device_id_type=MESH)
             return carry
 
-        lax.fori_loop(0, rows, one_row, 0)
-
-
-def rows_to_slots(rows, y_ref, to_slots_ref, mask_ref, out_ref):
-    for first in range(0, rows, GROUP_OUT):
-        freq = y_ref[first : first + GROUP_OUT].reshape(GROUP_OUT * FREQ, y_ref.shape[-1])
-        cells = product_split(to_slots_ref, freq).reshape(GROUP_OUT, SLOTS, y_ref.shape[-1])
-        out_ref[first : first + GROUP_OUT] = cells * mask_ref[first : first + GROUP_OUT]
-
-
-def conv_forward_kernel(
-    bounds, window, taps, mask, to_freq, taps_freq, to_slots, out, xf, kf, stats, yf
-):
-    rows = out.shape[0]
-    transform_window(window, to_freq, xf)
-    for first in range(0, kf.shape[0], GROUP_TAP):
-        part = taps[first : first + GROUP_TAP].reshape(GROUP_TAP * SPAN_PAD, taps.shape[-1])
-        freq = product_split(taps_freq, part)
-        kf[first : first + GROUP_TAP] = freq.reshape(GROUP_TAP, FREQ, freq.shape[-1])
-    sum_rows(bounds, rows, xf, kf, yf, False, True)
-    rows_to_slots(rows, yf, to_slots, mask, out)
-    cells = out[...].reshape(rows * SLOTS, out.shape[-1])
-    stats[0:1, :] = jnp.sum(cells, axis=0, keepdims=True)
-    stats[1:2, :] = jnp.sum(cells * cells, axis=0, keepdims=True)
-    stats[2:8, :] = jnp.zeros((6, stats.shape[-1]), F32)
-
-
-CHUNK = 256
-TAP_ROWS = 28
-
-
-def chunked(leading):
-    return pl.BlockSpec(leading + (CHUNK,), lambda c, *_: (0,) * len(leading) + (c,))
-
-
-def whole(array):
-    return pl.BlockSpec(array.shape, lambda c, *_: (0,) * array.ndim)
-
-
-def conv_forward(bounds, field, taps, mask):
-    window, _, channels = field.shape
-    rows = window - 2 * REACH
-    constants = [
-        jnp.asarray(split_constant(slots_to_freq(), GROUP_IN)),
-        jnp.asarray(split_constant(taps_to_freq(), GROUP_TAP)),
-        jnp.asarray(split_constant(freq_to_slots(), GROUP_OUT)),
-    ]
-    return pl.pallas_call(
-        conv_forward_kernel,
-        grid_spec=pltpu.PrefetchScalarGridSpec(
-            num_scalar_prefetch=1,
-            grid=(channels // CHUNK,),
-            in_specs=[
-                chunked((window, SLOTS)),
-                chunked((TAP_ROWS, SPAN_PAD)),
-                pl.BlockSpec((rows, SLOTS, CHUNK), lambda c, *_: (0, 0, 0)),
-            ]
-            + [whole(c) for c in constants],
-            out_specs=[
-                chunked((rows, SLOTS)),
-                chunked((window, FREQ)),
-                chunked((TAP_ROWS, FREQ)),
-                chunked((8,)),
-            ],
-            scratch_shapes=[
-                pltpu.VMEM((rows, FREQ, CHUNK), F32),
-            ],
-        ),
-        out_shape=[
-            jax.ShapeDtypeStruct((rows, SLOTS, channels), F32),
-            jax.ShapeDtypeStruct((window, FREQ, channels), F32),
-            jax.ShapeDtypeStruct((TAP_ROWS, FREQ, channels), F32),
-            jax.ShapeDtypeStruct((8, channels), F32),
-        ],
-        compiler_params=pltpu.CompilerParams(vmem_limit_bytes=36 << 20),
-        name="conv_forward",
-    )(bounds, field, taps, mask, *constants)
+        def greet_layer(step, carry):
+            pl.semaphore_signal(barrier, inc=1, device_id=self.layer(step), device_id_type=MESH)
+            return carry
+
+        lax.fori_loop(1, self.rows, greet_line, 0)
+        lax.fori_loop(1, self.count, greet_layer, 0)
+
+    def ready(self):
+        pl.semaphore_wait(pltpu.get_barrier_semaphore(), self.rows + self.count - 2)
+
+    def copy(self, src, dst, device):
+        made = pltpu.make_async_remote_copy(
+            src_ref=src,
+            dst_ref=dst,
+            send_sem=self.send_sem.at[self.used],
+            recv_sem=self.recv_sem.at[self.used],
+            device_id=device,
+            device_id_type=MESH,
+        )
+        self.used += 1
+        return made
+
+    def reserve(self, number):
+        self.used += number
+        return self.used - number
+
+    def copy_at(self, index, src, dst, device):
+        return pltpu.make_async_remote_copy(
+            src_ref=src,
+            dst_ref=dst,
+            send_sem=self.send_sem.at[index],
+            recv_sem=self.recv_sem.at[index],
+            device_id=device,
+            device_id_type=MESH,
+        )
+
+    def own(self, src, dst):
+        made = pltpu.make_async_copy(src, dst, self.recv_sem.at[self.used])
+        self.used += 1
+        return made
 
 
 def all_sum_job(net, value, out, line_slots, part, layer_slots):
@@ -240,104 +199,6 @@
     out[...] = total
 
 
-class Net:
-    def __init__(self, dp, rows, send_sem, recv_sem):
-        self.count, self.rows = dp, rows
-        self.send_sem, self.recv_sem, self.used = send_sem, recv_sem, 0
-        self.dp = lax.axis_index("dp")
-        self.z = lax.axis_index("rows")
-        self.bits = list(range(1, dp.bit_length() - 1))
-
-    def bit(self, index):
-        return lax.rem(self.dp // (1 << index), 2)
-
-    def across(self, index):
-        return (self.dp + (1 << index) * (1 - 2 * self.bit(index)), self.z)
-
-    def line(self, step):
-        return (self.dp, lax.rem(self.z + step, self.rows))
-
-    def layer(self, step):
-        return (lax.rem(self.dp + step, self.count), self.z)
-
-    def greet(self):
-        barrier = pltpu.get_barrier_semaphore()
-
-        def greet_line(step, carry):
-            pl.semaphore_signal(barrier, inc=1, device_id=self.line(step), device_id_type=MESH)
-            return carry
-
-        def greet_layer(step, carry):
-            pl.semaphore_signal(barrier, inc=1, device_id=self.layer(step), device_id_type=MESH)
-            return carry
-
-        lax.fori_loop(1, self.rows, greet_line, 0)
-        lax.fori_loop(1, self.count, greet_layer, 0)
-
-    def ready(self):
-        pl.semaphore_wait(pltpu.get_barrier_semaphore(), self.rows + self.count - 2)
-
-    def copy(self, src, dst, device):
-        made = pltpu.make_async_remote_copy(
-            src_ref=src,
-            dst_ref=dst,
-            send_sem=self.send_sem.at[self.used],
-            recv_sem=self.recv_sem.at[self.used],
-            device_id=device,
-            device_id_type=MESH,
-        )
-        self.used += 1
-        return made
-
-    def reserve(self, number):
-        self.used += number
-        return self.used - number
-
-    def copy_at(self, index, src, dst, device):
-        return pltpu.make_async_remote_copy(
-            src_ref=src,
-            dst_ref=dst,
-            send_sem=self.send_sem.at[index],
-            recv_sem=self.recv_sem.at[index],
-            device_id=device,
-            device_id_type=MESH,
-        )
-
-    def own(self, src, dst):
-        made = pltpu.make_async_copy(src, dst, self.recv_sem.at[self.used])
-        self.used += 1
-        return made
-
-
-def all_sum_job(net, value, out, line_slots, part, layer_slots):
-    own = net.own(value, line_slots.at[net.z])
-    own.start()
-    sent = [net.copy(value, line_slots.at[net.z], net.line(s)) for s in range(1, net.rows)]
-    for one in sent:
-        one.start()
-    yield
-    own.wait()
-    for one in sent:
-        one.wait()
-    total = line_slots[0]
-    for index in range(1, net.rows):
-        total = total + line_slots[index]
-    part[...] = total
-    own = net.own(part, layer_slots.at[net.dp])
-    own.start()
-    sent = [net.copy(part, layer_slots.at[net.dp], net.layer(s)) for s in range(1, net.count)]
-    for one in sent:
-        one.start()
-    yield
-    own.wait()
-    for one in sent:
-        one.wait()
-    total = layer_slots[0]
-    for index in range(1, net.count):
-        total = total + layer_slots[index]
-    out[...] = total
-
-
 def aligned(value, unit):
     return pl.multiple_of(value, unit)
 
@@ -365,18 +226,6 @@
     jobs = list(jobs)
     while jobs:
         jobs = [job for job in jobs if next(job, StopIteration) is not StopIteration]
-
-
-def line_gather_job(net, value, out):
-    own = net.own(value, out.at[net.z])
-    own.start()
-    sent = [net.copy(value, out.at[net.z], net.line(s)) for s in range(1, net.rows)]
-    for one in sent:
-        one.start()
-    yield
-    own.wait()
-    for one in sent:
-        one.wait()
 
 
 def sides(net, rows):
@@ -601,59 +450,6 @@
     return [pltpu.VMEM((rows, height, LANES), F32), pltpu.VMEM((height, LANES), F32), pltpu.VMEM((dp, height, LANES), F32)]
 
 
-def sums_names_weights(mesh, value, names, up, down):
-    rows = mesh[1]
-
-    def body(net, value, names, up, down, total, all_names, wall, *slots):
-        run(
-            weights_line_job(net, up, down, wall),
-            line_gather_job(net, names, all_names),
-            all_sum_job(net, value, total, *slots),
-        )
-
-    return exchange(
-        "sums_one",
-        0,
-        mesh,
-        body,
-        (value, names, up, down),
-        [VMEM] * 4,
-        [
-            shape(*value.shape),
-            jax.ShapeDtypeStruct((rows,) + names.shape, jnp.int32),
-            shape(rows, 2, *up.shape),
-        ],
-        [VMEM, VMEM, HBM],
-        sum_scratch(mesh, value.shape[0]),
-        16,
-    )
-
-
-def halo_weights(mesh, field, wall):
-    rows = field.shape[0]
-
-    def body(net, field, wall_in, window, wall, zeros):
-        halo = halo_job(net, field, window, zeros)
-        next(halo)
-        run(weights_layer_job(net, wall))
-        run(weights_pair_job(net, wall))
-        finish(halo)
-
-    return exchange(
-        "halo_act",
-        1,
-        mesh,
-        body,
-        (field, wall),
-        [VMEM, HBM],
-        [shape(rows + 2 * REACH, *field.shape[1:]), shape(*wall.shape)],
-        [HBM, HBM],
-        [pltpu.VMEM((REACH,) + field.shape[1:], F32)],
-        16,
-        {1: 1},
-    )
-
-
 def all_scratch(mesh, rows, width):
     size = (rows // 2 if width == 2 * LANES else rows) * 2 // mesh[0] // mesh[1]
     return [
@@ -749,21 +545,32 @@
 
 def middle_kernel(
     net,
-    conv,
+    conv_in,
     conv_sums,
+    x_in,
+    gy_in,
+    mask_in,
+    params,
+    total_one,
+    point_in,
+    wall_in,
+    delta_out,
+    back_out,
+    total_four,
+    total_five,
+    dconv_out,
+    point_out,
+    part,
+    wall,
     x,
     gy,
     mask,
-    params,
     point_two,
-    wall,
     delta,
     back,
-    total_four,
-    total_five,
     dconv,
     point_grad,
-    part,
+    load_sem,
     sums_own,
     sums_slots,
     own_sem,
@@ -788,13 +595,18 @@
     got_layer,
     got_line,
 ):
-    pixels, channels = conv.shape
+    pixels, channels = x.shape
     tiles = pixels // TILE
     hidden = w_up.shape[2]
     per_shard = wall.shape[2] // hidden
     chunks = net.rows * per_shard
     core = net.bit(0)
-    gain_two, bias_two, gain_three, bias_three, count = (params[row : row + 1, :] for row in range(5))
+    gain_two, bias_two, gain_three, bias_three = (params[row : row + 1, :] for row in range(4))
+    count = read_count(total_one)
+    loads = Loads(load_sem)
+    came_point = loads.start(point_in, point_two)
+    came_gy = loads.start(gy_in, gy)
+    came = [loads.start(src, dst) for src, dst in ((conv_in, xhat), (x_in, x), (mask_in, mask))]
 
     def each_tile(body):
         def one(index, carry):
@@ -824,18 +636,29 @@
     net.ready()
     job = total_job(0, sums_slots[1].at[0])
     next(job)
+
+    def weights_job():
+        yield from weights_layer_job(net, wall)
+        yield from weights_pair_job(net, wall)
+
+    weights = weights_job()
+    next(weights)
     for one in load(0):
         one.start()
+    came_point.wait()
     store_split(point_pair, Ellipsis, point_two[...])
+    came_gy.wait()
     store_split(g_pair, Ellipsis, gy[...])
     next(job)
     store_split(gt_pair, Ellipsis, gy[...].T)
     finish(job)
+    for one in came:
+        one.wait()
     mean, inv_two = norm_terms(sums_slots[1].at[0], count)
 
     def second_norm(rows, carry):
         m = valid(rows)
-        hat = (conv[rows, :] - mean) * inv_two
+        hat = (xhat[rows, :] - mean) * inv_two
         act, slope = gelu_parts((hat * gain_two + bias_two) * m)
         xhat[rows, :] = hat
         slope_two[rows, :] = slope * m
@@ -847,6 +670,7 @@
     write_sums(sums_own.at[1], *each_tile(second_norm))
     job = total_job(1, sums_slots[1].at[1])
     next(job)
+    next(weights)
     next(job)
     finish(job)
     mean_three, inv_three = norm_terms(sums_slots[1].at[1], count)
@@ -975,7 +799,7 @@
         for one in load(chunk):
             one.wait()
 
-        @pl.when(chunk + 1 < chunks)
+        @pl.when((chunk + 1 < chunks) & (chunk + 1 != per_shard))
         def _():
             for one in load(chunk + 1):
                 one.start()
@@ -1005,7 +829,16 @@
         each_tile(second_half)
         return carry
 
-    lax.fori_loop(0, chunks, feed_forward, 0)
+    lax.fori_loop(0, per_shard - 1, feed_forward, 0)
+    for _ in range(stages - 1):
+        next(weights)
+    lax.fori_loop(per_shard - 1, per_shard, feed_forward, 0)
+    finish(weights)
+    for one in load(per_shard):
+        one.start()
+    lax.fori_loop(per_shard, chunks, feed_forward, 0)
+
+    loads.leave(delta, delta_out)
 
     def third_sums(rows, carry):
         dy = back[rows, :] * valid(rows)
@@ -1036,12 +869,14 @@
         return carry[0] + column_sum(du), carry[1] + column_sum(du * xhat[rows, :])
 
     write_sums(sums_own.at[3], *each_tile(third_back))
+    loads.leave(back, back_out)
     job = total_job(3, total_five)
     next(job)
     for side in range(2):
         ut_pair[side][...] = act_pair[side][...].T
     next(job)
     point_grad[...] = dot_split(read_pair(ut_pair), read_pair(g_pair))
+    loads.leave(point_grad, point_out)
     finish(job)
     grad_bias_two, grad_gain_two = read_sums(total_five)
 
@@ -1052,6 +887,7 @@
         return carry
 
     lax.fori_loop(0, pixels // SLOTS, second_back, 0)
+    loads.leave(dconv, dconv_out)
     for chunk in range(chunks):
         for one in line_move(chunk, chunk >= per_shard):
             one.wait()
@@ -1061,9 +897,10 @@
             for index in range(1, net.rows):
                 total = total + got_line[index, block, which]
             part[which, block] = total
-
-
-def middle(mesh, conv, conv_sums, x, gy, mask, params, point_two, wall):
+    loads.finish()
+
+
+def middle(mesh, conv, conv_sums, x, gy, mask, params, total_one, point_two, wall):
     dp, rows = mesh
     pixels, channels = conv.shape
     hidden = 2 * LANES
@@ -1074,7 +911,18 @@
         return [pltpu.VMEM(dims, BF16)] * 2
 
     piece = channels * 2 // dp
+    field = pltpu.VMEM((pixels, channels), F32)
+    square = pltpu.VMEM((channels, channels), F32)
     scratch = [
+        field,
+        field,
+        pltpu.VMEM(mask.shape, F32),
+        square,
+        field,
+        field,
+        pltpu.VMEM((lines, SLOTS, channels), F32),
+        square,
+        pltpu.SemaphoreType.DMA((16,)),
         pltpu.VMEM((4, 8, LANES), F32),
         [pltpu.VMEM((4, rows, 8, LANES), F32), pltpu.VMEM((4, 8, LANES), F32), pltpu.VMEM((4, dp, 8, LANES), F32)],
         pltpu.SemaphoreType.DMA((3, 2)),
@@ -1104,15 +952,16 @@
         2,
         mesh,
         middle_kernel,
-        (conv, conv_sums, x, gy, mask, params, point_two, wall),
-        [VMEM] * 7 + [HBM],
+        (conv, conv_sums, x, gy, mask, params, total_one, point_two, wall),
+        [HBM, VMEM] + [HBM] * 3 + [VMEM] * 2 + [HBM] * 2,
         [shape(pixels, channels)] * 2
         + [shape(8, LANES)] * 2
         + [shape(lines, SLOTS, channels), shape(channels, channels)]
-        + [shape(2, wall.shape[2] // hidden, piece, LANES)],
-        [VMEM] * 7,
+        + [shape(2, wall.shape[2] // hidden, piece, LANES), shape(*wall.shape)],
+        [HBM] * 2 + [VMEM] * 2 + [HBM] * 2 + [VMEM, HBM],
         scratch,
         56,
+        {8: 7},
         late=True,
     )
 
@@ -1167,7 +1016,7 @@
                 for row in range(rows):
                     dr, di = d_ref[REACH + row, real, :], d_ref[REACH + row, imag, :]
                     for k in range(TAP_GROUP):
-                        w = table[side * SPAN + group * TAP_GROUP + k, row]
+                        w = table[side * rows + row, group * TAP_GROUP + k]
                         xr, xi = x_ref[w, real, :], x_ref[w, imag, :]
                         gr, gi = sums[k]
                         sums[k] = gr + (dr * xr + di * xi), gi + (dr * xi - di * xr)
@@ -1191,29 +1040,25 @@
     return [(down, below, above), (up, above, below)]
 
 
-def start_halo(net, field, window):
+def start_halo(net, field, window, index):
     rows = field.shape[0]
-    moves = [halo_moves(net, field, window, index) for index in range(window.shape[0])]
-    for block in moves:
-        for one, goes, _ in block:
-            pl.when(goes)(one.start)
+    moves = halo_moves(net, field, window, index)
+    for one, goes, _ in moves:
+        pl.when(goes)(one.start)
     empty = jnp.zeros((REACH,) + window.shape[2:], F32)
-    for index in range(window.shape[0]):
-        window[index, REACH : REACH + rows] = field[:, :, index * LANES : (index + 1) * LANES]
-        window[index, 2 * REACH + rows :] = jnp.zeros(
-            (window.shape[1] - 2 * REACH - rows,) + window.shape[2:], F32
-        )
-
-        @pl.when(net.z == 0)
-        def _():
-            window[index, :REACH] = empty
-
-        @pl.when(net.z == net.rows - 1)
-        def _():
-            window[index, REACH + rows : 2 * REACH + rows] = empty
-
-    def wait(index):
-        for one, goes, comes in moves[index]:
+    window[index, REACH : REACH + rows] = field[:, :, index * LANES : (index + 1) * LANES]
+    window[index, 2 * REACH + rows :] = jnp.zeros((window.shape[1] - 2 * REACH - rows,) + window.shape[2:], F32)
+
+    @pl.when(net.z == 0)
+    def _():
+        window[index, :REACH] = empty
+
+    @pl.when(net.z == net.rows - 1)
+    def _():
+        window[index, REACH + rows : 2 * REACH + rows] = empty
+
+    def wait():
+        for one, goes, comes in moves:
             pl.when(comes)(one.wait_recv)
             pl.when(goes)(one.wait_send)
 
@@ -1232,6 +1077,7 @@
     h_in,
     point_in,
     params,
+    total_one,
     back_in,
     part_in,
     point_grad_in,
@@ -1282,7 +1128,9 @@
     rows, _, channels = dconv.shape
     pixels = rows * SLOTS
     blocks = channels // LANES
-    gain, inv, count, mean, bias = (params[row : row + 1, :] for row in range(5))
+    gain, bias = params[0:1, :], params[1:2, :]
+    count = read_count(total_one)
+    mean, inv = norm_terms(total_one, count)
     loads = Loads(load_sem)
     came_dconv = loads.start(dconv_in, dconv)
     came_grad = loads.start(point_grad_in, point_grad)
@@ -1293,21 +1141,17 @@
     came_point = loads.start(point_in, point_one)
 
     def load_x(index):
-        return pltpu.make_async_copy(
-            xf.at[:, :, pl.ds(index * LANES, LANES)], x_block[index % 2].at[pl.ds(0, xf.shape[0])], own_sem.at[index % 2]
-        )
+        return pltpu.make_async_copy(xf.at[index], x_block[index % 2], own_sem.at[index % 2])
 
     def load_k(index):
-        return pltpu.make_async_copy(
-            kf.at[:, :, pl.ds(index * LANES, LANES)], k_block[index % 2], own_sem.at[2 + index % 2]
-        )
+        return pltpu.make_async_copy(kf.at[index], k_block[index % 2], own_sem.at[2 + index % 2])
 
     load_k(0).start()
     load_x(0).start()
     came_back = loads.start(back_in, back_three)
     came_dconv.wait()
     net.ready()
-    wait_halo = start_halo(net, dconv, window)
+    waits = [start_halo(net, dconv, window, index) for index in range(blocks)]
     came_grad.wait()
     came_part.wait()
 
@@ -1355,15 +1199,13 @@
 
     lax.fori_loop(0, pixels // LANES, prepare, 0)
     store_split(point_pair, Ellipsis, point_one[...])
-    for slot in range(2):
-        x_block[slot][ZERO_ROW:] = jnp.zeros((1,) + x_block[slot].shape[1:], F32)
     taps[:, SPAN * SPAN :, :] = jnp.zeros((taps.shape[0], taps.shape[1] - SPAN * SPAN, taps.shape[2]), F32)
 
-    for index in range(blocks):
+    def block_back(index):
         load_k(index).wait()
         if index + 1 < blocks:
             load_k(index + 1).start()
-        wait_halo(index)
+        waits[index]()
         lanes = slice(index * LANES, (index + 1) * LANES)
         transform(window.at[index], to_freq, df.at[index], to_freq.shape[0] // FREQ)
         sum_table(row_table, rows, df.at[index], k_block[index % 2], yf, True)
@@ -1372,22 +1214,8 @@
             where = slice(first * SLOTS, (first + group) * SLOTS)
             dact = product_split(to_slots, yf[first : first + group].reshape(group * FREQ, LANES))
             dh_pair[0][where, lanes], dh_pair[1][where, lanes] = split_two(dact * slope[where, lanes])
-    progress()
-    one_grad[...] = dot_split(read_pair(ut_pair), read_pair(dh_pair))
-    background.append(then(reduce_all_job(net, one_grad, *one_scratch, grad_one), lambda: loads.leave(grad_one, one_out)))
-    progress()
-
-    def last_sums(index, carry):
-        where = pl.ds(aligned(index * TILE, TILE), TILE)
-        dy = dot_split(read_pair(dh_pair, where), read_pair(point_pair), NT) * valid(where)
-        du[where, :] = dy
-        return carry[0] + column_sum(dy), carry[1] + column_sum(dy * xhat[where, :])
-
-    zero = jnp.zeros((1, channels), F32)
-    write_sums(sums_own, *lax.fori_loop(0, pixels // TILE, last_sums, (zero, zero)))
-    background.append(all_sum_job(net, sums_own, total, *sums_slots))
-    progress()
-    for index in range(blocks):
+
+    def block_taps(index):
         load_x(index).wait()
         if index + 1 < blocks:
             load_x(index + 1).start()
@@ -1402,7 +1230,33 @@
         if index % 2:
             job = reduce_all_job(net, taps.at[half], *taps_scratch[half], taps_flat[half])
             background.append(then(job, functools.partial(keep_taps, half)))
+
+    early = blocks // 2
+    for index in range(blocks):
+        block_back(index)
+        if 1 <= index <= early:
+            block_taps(index - 1)
         progress()
+    one_grad[...] = dot_split(read_pair(ut_pair), read_pair(dh_pair))
+    job = reduce_all_job(net, one_grad, *one_scratch, grad_one)
+    background.append(then(job, lambda: loads.leave(grad_one, one_out)))
+    progress()
+
+    def last_sums(index, carry):
+        where = pl.ds(aligned(index * TILE, TILE), TILE)
+        dy = dot_split(read_pair(dh_pair, where), read_pair(point_pair), NT) * valid(where)
+        du[where, :] = dy
+        return carry[0] + column_sum(dy), carry[1] + column_sum(dy * xhat[where, :])
+
+    zero = jnp.zeros((1, channels), F32)
+    write_sums(sums_own, *lax.fori_loop(0, pixels // TILE, last_sums, (zero, zero)))
+    sums = all_sum_job(net, sums_own, total, *sums_slots)
+    next(sums)
+    for index in range(early, blocks):
+        block_taps(index)
+        progress()
+        next(sums, None)
+    finish(sums)
     grad_bias, grad_gain = read_sums(total)
     came_back.wait()
 
@@ -1459,7 +1313,7 @@
         one.wait()
 
 
-def last(mesh, tables, dconv, xf, kf, mask, x, hidden, point_one, params, back_three, part, point_grad):
+def last(mesh, tables, dconv, xf, kf, mask, x, hidden, point_one, params, total_one, back_three, part, point_grad):
     dp, rows = mesh
     lines, _, channels = dconv.shape
     pixels = lines * SLOTS
@@ -1518,8 +1372,8 @@
         3,
         mesh,
         last_kernel,
-        (*tables, dconv, xf, kf, mask, x, hidden, point_one, params, back_three, part, point_grad, *constants),
-        [smem] * 2 + [HBM] * 7 + [VMEM] + [HBM] * 3 + [VMEM] * 3,
+        (*tables, dconv, xf, kf, mask, x, hidden, point_one, params, total_one, back_three, part, point_grad, *constants),
+        [smem] * 2 + [HBM] * 7 + [VMEM] * 2 + [HBM] * 3 + [VMEM] * 3,
         [shape(pixels, channels), shape(8, LANES)] + [shape(channels, channels)] * 4 + [shape(SPAN, SPAN, channels)],
         [HBM, VMEM] + [HBM] * 5,
         scratch,
@@ -1528,16 +1382,251 @@
     )
 
 
-def product(left, right):
-    return jnp.dot(left, right, precision=HIGH, preferred_element_type=F32)
-
-
-def product_t(left, right):
-    return lax.dot_general(left, right, (((1,), (1,)), ((), ())), precision=HIGH, preferred_element_type=F32)
-
-
-def contract(left, right):
-    return lax.dot_general(left, right, (((0,), (0,)), ((), ())), precision=HIGH, preferred_element_type=F32)
+def first_kernel(
+    net,
+    value,
+    names,
+    x_in,
+    up_in,
+    down_in,
+    point_in,
+    taps_in,
+    mask_in,
+    params,
+    to_freq,
+    taps_freq,
+    to_slots,
+    hidden_out,
+    wall,
+    xf_out,
+    kf_out,
+    conv_out,
+    conv_sums,
+    total,
+    row_table,
+    tap_table,
+    x,
+    up,
+    down,
+    point_one,
+    taps,
+    mask,
+    load_sem,
+    sums_slots,
+    got_names,
+    name_rows,
+    u_pair,
+    point_pair,
+    hidden,
+    act,
+    window,
+    xf,
+    kf,
+    yf,
+    conv,
+):
+    rows, _, channels = act.shape
+    pixels = rows * SLOTS
+    blocks = channels // LANES
+    gain, bias = params[0:1, :], params[1:2, :]
+    loads = Loads(load_sem)
+    came_up = loads.start(up_in, up)
+    came_down = loads.start(down_in, down)
+    came_x = loads.start(x_in, x)
+    came_point = loads.start(point_in, point_one)
+    came_mask = loads.start(mask_in, mask)
+    came_taps = loads.start(taps_in, taps)
+    net.ready()
+    sums = all_sum_job(net, value, total, *sums_slots)
+    next(sums)
+    below, above = net.z < net.rows - 1, net.z > 0
+    name_moves = [
+        (net.copy(names.at[1], got_names.at[0], net.line(1)), below, above),
+        (net.copy(names.at[2], got_names.at[1], net.line(net.rows - 1)), above, below),
+    ]
+    for one, goes, _ in name_moves:
+        pl.when(goes)(one.start)
+
+    @pl.when(net.z == 0)
+    def _():
+        got_names[0] = jnp.zeros(got_names.shape[1:], jnp.int32)
+
+    @pl.when(net.z == net.rows - 1)
+    def _():
+        got_names[1] = jnp.zeros(got_names.shape[1:], jnp.int32)
+
+    came_up.wait()
+    came_down.wait()
+
+    background = [weights_line_job(net, up, down, wall)]
+
+    def progress():
+        background[:] = [job for job in background if next(job, StopIteration) is not StopIteration]
+
+    progress()
+    next(sums)
+    came_point.wait()
+    store_split(point_pair, Ellipsis, point_one[...])
+    came_x.wait()
+    came_mask.wait()
+    finish(sums)
+    progress()
+    mean, inv = norm_terms(total, read_count(total))
+
+    def first_norm(index, carry):
+        where = pl.ds(aligned(index * LANES, LANES), LANES)
+        m = jnp.concatenate([mask[where, :]] * blocks, axis=1)
+        store_split(u_pair, where, ((x[where, :] - mean) * inv * gain + bias) * m)
+        return carry
+
+    lax.fori_loop(0, pixels // LANES, first_norm, 0)
+    waits = []
+    for half in range(blocks // 2):
+        lanes = slice(half * 2 * LANES, (half + 1) * 2 * LANES)
+        for tile in range(pixels // TILE):
+            where = slice(tile * TILE, (tile + 1) * TILE)
+            pre = dot_split(
+                (u_pair[0][where, :], u_pair[1][where, :]), (point_pair[0][:, lanes], point_pair[1][:, lanes])
+            )
+            hidden[where, lanes] = pre
+            act[where.start // SLOTS : where.stop // SLOTS, :, lanes] = gelu_parts(pre)[0].reshape(
+                TILE // SLOTS, SLOTS, 2 * LANES
+            )
+        waits += [start_halo(net, act, window, index) for index in (2 * half, 2 * half + 1)]
+    loads.leave(hidden, hidden_out)
+    came_taps.wait()
+    group = taps_freq.shape[0] // FREQ
+    for index in range(blocks):
+        for first in range(0, taps.shape[0], group):
+            part = taps[first : first + group, :, index * LANES : (index + 1) * LANES]
+            freq = product_split(taps_freq, part.reshape(group * SPAN_PAD, LANES))
+            kf[index][first : first + group] = freq.reshape(group, FREQ, LANES)
+        loads.leave(kf[index], kf_out.at[index])
+    for one, goes, comes in name_moves:
+        pl.when(comes)(one.wait_recv)
+        pl.when(goes)(one.wait_send)
+    moved = [loads.start(src, name_rows.at[k]) for k, src in enumerate((names.at[0], got_names.at[0], got_names.at[1]))]
+    for one in moved:
+        one.wait()
+    list_rows(rows, name_rows, row_table, tap_table)
+    sums = [jnp.zeros((1, LANES), F32)] * 2 * blocks
+    for index in range(blocks):
+        lanes = slice(index * LANES, (index + 1) * LANES)
+        waits[index]()
+        transform(window.at[index], to_freq, xf[index], to_freq.shape[0] // FREQ)
+        loads.leave(xf[index].at[pl.ds(0, ZERO_ROW + 1)], xf_out.at[index])
+        sum_table(row_table, rows, xf[index], kf[index], yf, False)
+        group = to_slots.shape[0] // SLOTS
+        for first in range(0, rows, group):
+            where = slice(first * SLOTS, (first + group) * SLOTS)
+            cells = product_split(to_slots, yf[first : first + group].reshape(group * FREQ, LANES)) * mask[where, :]
+            conv[where, lanes] = cells
+            sums[2 * index] = sums[2 * index] + column_sum(cells)
+            sums[2 * index + 1] = sums[2 * index + 1] + column_sum(cells * cells)
+        if index == 0:
+            progress()
+    loads.leave(conv, conv_out)
+    for index in range(blocks):
+        conv_sums[index : index + 1, :] = sums[2 * index]
+        conv_sums[4 + index : 5 + index, :] = sums[2 * index + 1]
+    while background:
+        progress()
+    loads.finish()
+
+
+def list_rows(rows, names, row_table, tap_table):
+    for side in range(2):
+
+        def name(w):
+            return names[0, side, w] + names[1, side, w] + names[2, side, w]
+
+        def one_row(row, carry):
+            at = row + REACH
+            own = name(at)
+
+            def count(first):
+                same = jnp.int32(0)
+                for k in range(REACH):
+                    same = same + jnp.where(name(first + k) == own, 1, 0)
+                return same
+
+            low = at - count(row)
+            high = jnp.where(own > 0, at + 1 + count(at + 1), low)
+            for tap in range(LEFT_TAPS):
+                row_table[side * rows + row, tap] = jnp.where(low + tap < high, low + tap, ZERO_ROW)
+            for tap in range(SPAN):
+                w = row + tap
+                tap_table[side * rows + row, tap] = jnp.where((w >= low) & (w < high), w, ZERO_ROW)
+            return carry
+
+        lax.fori_loop(0, rows, one_row, 0)
+
+
+def read_count(total):
+    return jnp.concatenate([total[8 + row : 9 + row, :] for row in range(4)], axis=1)
+
+
+def first(mesh, value, names, x, up, down, point_one, taps, mask, params):
+    dp, devices = mesh
+    pixels, channels = x.shape
+    lines = pixels // SLOTS
+    blocks = channels // LANES
+    constants = [
+        jnp.asarray(split_constant(slots_to_freq(), 2)),
+        jnp.asarray(split_constant(taps_to_freq(), 4)),
+        jnp.asarray(split_constant(freq_to_slots(), 2)),
+    ]
+
+    def pair(*dims):
+        return [pltpu.VMEM(dims, BF16)] * 2
+
+    field = pltpu.VMEM((pixels, channels), F32)
+    scratch = [
+        field,
+        pltpu.VMEM(up.shape, F32),
+        pltpu.VMEM(down.shape, F32),
+        pltpu.VMEM(point_one.shape, F32),
+        pltpu.VMEM(taps.shape, F32),
+        pltpu.VMEM(mask.shape, F32),
+        pltpu.SemaphoreType.DMA((24,)),
+        sum_scratch(mesh, value.shape[0]),
+        pltpu.VMEM((2, 8, LANES), jnp.int32),
+        pltpu.SMEM((3, 8, LANES), jnp.int32),
+        pair(pixels, channels),
+        pair(channels, channels),
+        field,
+        pltpu.VMEM((lines, SLOTS, channels), F32),
+        pltpu.VMEM((blocks, WINDOW_PAD, SLOTS, LANES), F32),
+        [pltpu.VMEM((WINDOW_PAD, FREQ, LANES), F32)] * blocks,
+        [pltpu.VMEM((TAP_ROWS, FREQ, LANES), F32)] * blocks,
+        pltpu.VMEM((lines, FREQ, LANES), F32),
+        field,
+    ]
+    smem = pl.BlockSpec(memory_space=pltpu.SMEM)
+    table = jax.ShapeDtypeStruct((2 * lines, LANES), jnp.int32)
+    return exchange(
+        "first",
+        0,
+        mesh,
+        first_kernel,
+        (value, names, x, up, down, point_one, taps, mask, params, *constants),
+        [VMEM, VMEM] + [HBM] * 6 + [VMEM] * 4,
+        [
+            shape(pixels, channels),
+            shape(devices, 2, *up.shape),
+            shape(blocks, ZERO_ROW + 1, FREQ, LANES),
+            shape(blocks, TAP_ROWS, FREQ, LANES),
+            shape(pixels, channels),
+            shape(8, LANES),
+            shape(*value.shape),
+            table,
+            table,
+        ],
+        [HBM] * 5 + [VMEM] * 2 + [smem] * 2,
+        scratch,
+        48,
+        late=True,
+    )
 
 
 def shards(
@@ -1617,74 +1706,66 @@
     def sums(field):
         return jnp.sum(field, axis=0), jnp.sum(field * field, axis=0)
 
-    names = jnp.stack([left_id, right_id], axis=1) + 1
-    names_tile = jnp.pad(names.reshape(1, 2 * rows), ((0, 7), (0, LANES - 2 * rows)))
+    names = jnp.stack([left_id, right_id]) + 1
+
+    def name_tile(first, last, lane):
+        return jnp.pad(names[:, first:last], ((0, 6), (lane, LANES - lane - (last - first))))
+
+    names = jnp.stack(
+        [
+            name_tile(0, rows, REACH),
+            name_tile(rows - REACH, rows, 0),
+            name_tile(0, REACH, REACH + rows),
+        ]
+    )
     x = compact(inputs)
     gy = compact(out_grad)
-    total, all_names, wall = sums_names_weights(
-        mesh,
-        jnp.concatenate([pack(*sums(x)), pack(jnp.full((channels,), jnp.sum(valid)), jnp.zeros((channels,)))]),
-        names_tile,
-        w_up,
-        w_down,
-    )
-    count = total[8, 0]
-    total = total[:8].reshape(2, channels)
-    all_names = jnp.pad(all_names[:, 0, : 2 * rows].reshape(devices_rows * rows, 2), ((REACH, REACH), (0, 0)))
-    window_rows = rows + 2 * REACH
-    window_names = lax.dynamic_slice_in_dim(all_names, lax.axis_index("rows") * rows, window_rows, 0)
-    w_index = jnp.arange(window_rows, dtype=jnp.int32)[None, :]
-    r_index = jnp.arange(rows, dtype=jnp.int32)[:, None]
-    near = (w_index >= r_index) & (w_index <= r_index + 2 * REACH)
-    bounds = []
-    for which in range(2):
-        same = near & (names[:, which][:, None] == window_names[:, which][None, :]) & (names[:, which][:, None] > 0)
-        low = jnp.min(jnp.where(same, w_index, window_rows), axis=1)
-        high = jnp.max(jnp.where(same, w_index + 1, 0), axis=1)
-        bounds += [jnp.minimum(low, high), high]
-    bounds = jnp.stack(bounds).astype(jnp.int32)
-    low, high = bounds[0::2][:, :, None], bounds[1::2][:, :, None]
-    listed = low + jnp.arange(LEFT_TAPS, dtype=jnp.int32)
-    row_table = jnp.where(listed < high, listed, ZERO_ROW).reshape(2 * rows, LEFT_TAPS)
-    listed = jnp.arange(rows, dtype=jnp.int32)[:, None] + jnp.arange(SPAN, dtype=jnp.int32)
-    listed = jnp.where((listed >= low) & (listed < high), listed, ZERO_ROW)
-    tables = (row_table, listed.transpose(0, 2, 1).reshape(2 * SPAN, rows))
-
-    mask = slot_mask.reshape(pixels, 1)
-    mask_wide = jnp.broadcast_to(slot_mask[:, :, None], (rows, SLOTS, CHUNK))
-
-    def norm_scale(total):
-        mean = total[0] / count
-        return mean, lax.rsqrt(total[1] / count - mean * mean + EPSILON)
-
-    mean_one, inv_one = norm_scale(total)
-    xhat_one = (x - mean_one) * inv_one
-    u1 = (xhat_one * first_norm_gain + first_norm_bias) * mask
-    h1 = product(u1, point_one)
-    act, act_slope = gelu_parts(h1)
-    act = act.reshape(rows, SLOTS, channels)
+    mask_lanes = jnp.broadcast_to(slot_mask.reshape(pixels, 1), (pixels, LANES))
     small_start = REACH - kernel_small.shape[0] // 2
     edge = (small_start, small_start)
     kernel = kernel_big + jnp.pad(kernel_small, (edge, edge, (0, 0)))
     taps = jnp.pad(kernel, ((0, TAP_ROWS - SPAN), (0, SPAN_PAD - SPAN), (0, 0)))
-    act_window, wall = halo_weights(mesh, act, wall)
-    conv, xf, kf, conv_sums = conv_forward(bounds, act_window, taps, mask_wide)
-    conv = conv.reshape(pixels, channels)
-    conv_sums = conv_sums[:2].reshape(8, LANES)
-    vectors = [second_norm_gain, second_norm_bias, feedforward_norm_gain, feedforward_norm_bias]
-    params = jnp.stack(vectors + [jnp.full((channels,), count)] + [jnp.zeros((channels,), F32)] * 3)
-    mask_lanes = jnp.broadcast_to(mask, (pixels, LANES))
-    delta, back_three, total_four, total_five, dconv, point_grad, part = middle(
-        mesh, conv, conv_sums, x, gy, mask_lanes, params, point_two, wall
+    vectors = [
+        first_norm_gain,
+        first_norm_bias,
+        second_norm_gain,
+        second_norm_bias,
+        feedforward_norm_gain,
+        feedforward_norm_bias,
+    ]
+    params = jnp.pad(jnp.stack(vectors), ((0, 10), (0, 0)))
+    hidden, wall, xf, kf, conv, conv_sums, total_one, *tables = first(
+        mesh,
+        jnp.concatenate([pack(*sums(x)), pack(jnp.full((channels,), jnp.sum(valid)), jnp.zeros((channels,)))]),
+        names,
+        x,
+        w_up,
+        w_down,
+        point_one,
+        taps,
+        mask_lanes,
+        params[0:8],
+    )
+    delta, back_three, total_four, total_five, dconv, point_grad, part, _ = middle(
+        mesh, conv, conv_sums, x, gy, mask_lanes, params[2:10], total_one, point_two, wall
     )
     grad_bias_three, grad_gain_three = total_four.reshape(2, channels)
     grad_bias_two, grad_gain_two = total_five.reshape(2, channels)
-    params = jnp.stack(
-        [first_norm_gain, inv_one, jnp.full((channels,), count), mean_one, first_norm_bias]
-        + [jnp.zeros((channels,), F32)] * 3
-    )
     cells, total, grad_point_one, grad_point_two, grad_up, grad_down, grad_kernel = last(
-        mesh, tables, dconv, xf, kf, mask_lanes, x, h1, point_one, params, back_three, part, point_grad
+        mesh,
+        tables,
+        dconv,
+        xf,
+        kf,
+        mask_lanes,
+        x,
+        hidden,
+        point_one,
+        params[0:8],
+        total_one,
+        back_three,
+        part,
+        point_grad,
     )
     grad_bias_one, grad_gain_one = total.reshape(2, channels)
     output = inputs + expand(delta)

time: 363 us -> 307 us (0.85)
  Pallas kernels: 298 us -> 261 us
  local copies, waits for them, and re-layouts: 35.8 us -> 26 us
  matrix products: 14.4 us -> 8.79 us
    pallas_call x1 -> x0, Pallas kernels: 19.2 us -> none  [conv_forward(): pl.pallas_call(conv_forward_kernel, grid_spec=pltpu.PrefetchScalarGridSpe...]
    pallas_call x4 -> x3, Pallas kernels: 279 us -> 261 us  [exchange(): pl.pallas_call(kernel, out_shape=outs, in_specs=in_specs, out_specs=out_s...]
    unnamed x65 -> x59, local copies, waits for them, and re-layouts: 26.4 us -> 17.7 us
    dot_general x1 -> x0, matrix products: 3.87 us -> none  [product(): return jnp.dot(left, right, precision=HIGH, preferred_element_type=F32)]
where the time goes in v1:
time: 307 us; the launch traced here: 303 us
  Pallas kernels  261 us (85%)
  local copies, waits for them, and re-layouts  26 us (8%)
  matrix products  8.79 us (3%)
  other arithmetic  5.41 us (2%)
    pallas_call x3, Pallas kernels, exchange(): pl.pallas_call(kernel, out_shape=outs, in_specs=in_specs, out_specs=out_s...  261 us
    unnamed x59, local copies, waits for them, and re-layouts  17.7 us

profile of v1, /device:TPU:0, one launch (start us, length us, event | category | flops | bytes accessed | tf_op | source)
XLA Modules:
  0.0 302.9 jit_solution(1779443134248207974)
XLA Ops:
  0.6 1.3 convert_reduce_fusion.1
  2.0 0.6 stack.63
  2.7 0.1 reshape.100
  2.8 0.1 pad.37.clone
  2.8 0.8 select_reduce_fusion.1
  3.7 0.1 fusion.15
  3.8 0.1 pad_bitcast_fusion.2
  3.9 0.1 pad_bitcast_fusion
  4.2 0.1 broadcast_compare_fusion
  4.2 0.1 pad_add_fusion.3
  4.4 0.1 pad_add_fusion.2
  4.5 1.1 convert_reduce_fusion
  5.6 0.1 broadcast_in_dim.62
  5.7 0.8 stack.80
  6.5 0.6 pad_slice_fusion
  7.1 0.1 broadcast_in_dim.63.refs_7_.refs_4_.refs_5_
  7.3 3.5 %fusion = f32[16,40,512]{2,1,0:T(8,128)} fusion(f32[16,1,44,512]{3,1,2,0:T(1,128)} %param.35, s32[16,40]{1,0:T(8,128)S(1)} %pad_add_fusion.3, s32[16,44]{1,0:T(8,128)} %bitcast.59, s32[16,40]{1,0:T(8,128)S(1)} %pad_add_fusion.2, pred[16,40]{1,0:T(8,128)(4,1)S(1)} %broadcast_compare_fusion), kind=kOutput, calls=%fused_computation.3 | convolution fusion | flops 173127680 | bytes 2761088 | tf_op jit(solution)/shard_map/dot_general | solution.py:1689
  10.8 2.0 fusion.14
  12.9 1.6 pad_add_fusion
  14.6 1.4 pad.29.refs_6_
  16.0 0.7 copy-done.3
  16.7 0.3 copy-done.4
  17.0 0.1 copy-done.7
  17.1 58.8 %first.1 = (f32[640,512]{1,0:T(8,128)S(1)}, f32[4,2,512,512]{3,2,1,0:T(8,128)}, f32[4,43,80,128]{3,2,1,0:T(8,128)}, f32[4,28,80,128]{3,2,1,0:T(8,128)}, f32[640,...) custom-call(f32[16,128]{1,0:T(8,128)S(1)} %pad_maximum_fusion.refs_0, ...), custom_call_target="tpu_custom_call" | custom-call | tf_op jit(solution)/shard_map/first/pallas_call | solution.py:434
  76.0 1.0 copy-done.2
  77.0 0.6 copy-done.9
  77.6 0.6 copy-done.10
  78.2 0.6 copy-done.11
  78.8 0.6 copy-done.12
  79.4 110.8 %middle.1 = (f32[640,512]{1,0:T(8,128)}, f32[640,512]{1,0:T(8,128)}, f32[8,128]{1,0:T(8,128)}, f32[8,128]{1,0:T(8,128)}, f32[16,40,512]{2,1,0:T(8,128)}, /*index...) custom-call(f32[640,512]{1,0:T(8,128)} %get-tuple-element.37.refs_0_, ...), custom_call_target="tpu_custom_call", output_to_operand_aliasing={{7}: (8, {})} | custom-call | tf_op jit(solution)/shard_map/middle/pallas_call | solution.py:434
  190.2 91.8 %last.1 = (f32[640,512]{1,0:T(8,128)}, f32[8,128]{1,0:T(8,128)}, f32[512,512]{1,0:T(8,128)}, f32[512,512]{1,0:T(8,128)}, f32[512,512]{1,0:T(8,128)}, /*index=5*/f32[512,512]{1,0:T(8,128)}, f32[27,27,512]{2,1,0:T(8,128)}) custom-call(s32[32,128]{1,0:T(8,128)} %copy-done.10, s32[32,128]{1,0:T(8,128)} %copy-done.11, f32[16,40,512]{2,1,0:T(8,128)} %get-tuple-element.44.refs_2_, ...), custom_call_target="tpu_custom_call" | custom-call | tf_op jit(solution)/shard_map/last/pallas_call | solution.py:434
  282.0 1.3 slice_bitcast_fusion.4
  283.3 0.6 slice_bitcast_fusion.2
  283.9 0.6 slice_bitcast_fusion
  284.5 1.5 slice.26
  286.0 1.7 bitcast_add_fusion.1
  287.7 2.6 copy.46
  290.3 1.7 bitcast_add_fusion
  292.0 2.6 copy.47
  294.6 1.0 copy.68
  295.5 0.9 copy-done.15
  296.4 1.2 copy.69
  297.6 0.7 copy-done.20
  298.3 1.0 copy.70
  299.3 0.6 copy-done.19
  299.9 1.0 copy.71
  300.9 0.6 copy-done.18
  301.5 1.0 copy.72
  (51 shorter events, 0.6 us)
Async XLA Ops:
  7.1 8.9 %copy-start.8 = (f32[8,512]{1,0:T(8,128)}, f32[8,512]{1,0:T(8,128)S(1)}, u32[]{:S(2)}) copy-start(f32[8,512]{1,0:T(8,128)S(1)} %get-tuple-element.95.refs_8_.refs_9_) | copy-start | bytes 49156
  7.2 8.8 %copy-start = (f32[640,128]{1,0:T(8,128)}, f32[640,128]{1,0:T(8,128)S(1)}, u32[]{:S(2)}) copy-start(f32[640,128]{1,0:T(8,128)S(1)} %broadcast_in_dim.63.refs_7_.refs_4_.refs_5_) | copy-start | bytes 983044
  7.3 3.5 %copy-start.13 = (f32[16,1,44,512]{3,1,2,0:T(1,128)S(1)}, f32[16,1,44,512]{3,1,2,0:T(1,128)}, u32[]{:S(2)}) copy-start(f32[16,1,44,512]{3,1,2,0:T(1,128)} %param.21) | copy-start | bytes 4325380
  7.3 3.5 %copy-start.22 = (s32[16,1,44]{2,1,0:T(1,128)S(1)}, s32[16,1,44]{2,1,0:T(1,128)}, u32[]{:S(2)}) copy-start(s32[16,1,44]{2,1,0:T(1,128)} %param.22) | copy-start | bytes 8452
  10.8 2.1 copy-start.23
  14.5 1.5 copy-start.1
  14.5 2.2 copy-start.3
  14.5 2.5 copy-start.4
  14.6 2.5 copy-start.5
  14.6 2.5 copy-start.6
  14.6 2.5 copy-start.7
  76.0 1.1 copy-start.2
  77.0 0.6 copy-start.9
  77.6 0.6 copy-start.10
  78.2 0.6 copy-start.11
  78.8 0.6 copy-start.12
  190.2 93.2 %copy-start.25 = (f32[8,128]{1,0:T(8,128)S(1)}, f32[8,128]{1,0:T(8,128)}, u32[]{:S(2)}) copy-start(f32[8,128]{1,0:T(8,128)} %get-tuple-element.55) | copy-start | bytes 12292
  190.2 93.7 %copy-start.24 = (f32[8,128]{1,0:T(8,128)S(1)}, f32[8,128]{1,0:T(8,128)}, u32[]{:S(2)}) copy-start(f32[8,128]{1,0:T(8,128)} %get-tuple-element.57) | copy-start | bytes 12292
  190.2 95.8 %copy-start.16 = (f32[640,512]{1,0:T(8,128)S(1)}, f32[640,512]{1,0:T(8,128)}, u32[]{:S(2)}) copy-start(f32[640,512]{1,0:T(8,128)} %get-tuple-element.41) | copy-start | bytes 3932164
  287.7 2.6 copy-start.14
  287.7 2.6 copy-start.17
  292.0 2.6 copy-start.21
  294.6 1.9 copy-start.15
  296.4 1.9 copy-start.20
  298.3 1.6 copy-start.19
  299.9 1.6 copy-start.18

commit v2 on v1

--- a/solution.py
+++ b/solution.py
@@ -264,21 +264,23 @@
         one.wait()
 
 
-def weights_layer_job(net, wall):
+def weights_layer_job(net, wall, distances):
     parts = sides(net, wall.shape[2])
+    shards = [net.z + way * distance for distance in distances for way in (1, -1)]
+    shards = [(lax.rem(shard + net.rows, net.rows), (shard >= 0) & (shard < net.rows)) for shard in shards]
     for back in range(1, len(net.bits) + 1):
         moves = []
         for lanes, steps, _, _ in parts:
             bit, base, rows = steps[-back]
             mine = pl.ds(aligned(base + net.bit(bit) * (rows // 2), 8), rows // 2)
-            for step in range(1, net.rows):
-                piece = wall.at[lax.rem(net.z + step, net.rows), :, mine, lanes]
-                moves.append(net.copy(piece, piece, net.across(bit)))
-        for one in moves:
-            one.start()
+            for shard, there in shards:
+                piece = wall.at[shard, :, mine, lanes]
+                moves.append((net.copy(piece, piece, net.across(bit)), there))
+        for one, there in moves:
+            pl.when(there)(one.start)
         yield
-        for one in moves:
-            one.wait()
+        for one, there in moves:
+            pl.when(there)(one.wait)
 
 
 def weights_pair_job(net, wall):
@@ -601,7 +603,7 @@
     per_shard = wall.shape[2] // hidden
     chunks = net.rows * per_shard
     core = net.bit(0)
-    gain_two, bias_two, gain_three, bias_three = (params[row : row + 1, :] for row in range(4))
+    gain_two, bias_two, gain_three, bias_three = (params[row : row + 1, :] for row in range(2, 6))
     count = read_count(total_one)
     loads = Loads(load_sem)
     came_point = loads.start(point_in, point_two)
@@ -638,7 +640,7 @@
     next(job)
 
     def weights_job():
-        yield from weights_layer_job(net, wall)
+        yield from weights_layer_job(net, wall, range(2, net.rows))
         yield from weights_pair_job(net, wall)
 
     weights = weights_job()
@@ -807,26 +809,24 @@
         store_split(up_pair, Ellipsis, w_up[slot])
         store_split(down_pair, Ellipsis, w_down[slot])
 
-        def first_half(rows, carry):
+        def first_half(rows):
             hid, slope = gelu_parts(dot_split(read_pair(u_pair, rows), read_pair(up_pair)))
             store_split(hid_pair, rows, hid)
             store_split(
                 dpre_pair, rows, dot_split(read_pair(g_pair, rows), read_pair(down_pair), NT) * slope
             )
-            return carry
-
-        each_tile(first_half)
+
+        first_half(pl.ds(0, pixels))
         made[slot, 0] = dot_split(read_pair(ut_pair), read_pair(dpre_pair))
         made[slot, 1] = dot_split(read_pair(gt_pair), read_pair(hid_pair))
         for one in pair_move(chunk):
             one.start()
 
-        def second_half(rows, carry):
+        def second_half(rows):
             delta[rows, :] += dot_split(read_pair(hid_pair, rows), read_pair(down_pair))
             back[rows, :] += dot_split(read_pair(dpre_pair, rows), read_pair(up_pair), NT)
-            return carry
-
-        each_tile(second_half)
+
+        second_half(pl.ds(0, pixels))
         return carry
 
     lax.fori_loop(0, per_shard - 1, feed_forward, 0)
@@ -1205,9 +1205,7 @@
         load_k(index).wait()
         if index + 1 < blocks:
             load_k(index + 1).start()
-        waits[index]()
         lanes = slice(index * LANES, (index + 1) * LANES)
-        transform(window.at[index], to_freq, df.at[index], to_freq.shape[0] // FREQ)
         sum_table(row_table, rows, df.at[index], k_block[index % 2], yf, True)
         group = to_slots.shape[0] // SLOTS
         for first in range(0, rows, group):
@@ -1219,6 +1217,8 @@
         load_x(index).wait()
         if index + 1 < blocks:
             load_x(index + 1).start()
+        waits[index]()
+        transform(window.at[index], to_freq, df.at[index], to_freq.shape[0] // FREQ)
         sum_taps(tap_table, rows, df.at[index], x_block[index % 2], gf)
         group = to_taps.shape[0] // SPAN_PAD
         half, lanes = index // 2, slice(index % 2 * LANES, (index % 2 + 1) * LANES)
@@ -1231,15 +1231,25 @@
             job = reduce_all_job(net, taps.at[half], *taps_scratch[half], taps_flat[half])
             background.append(then(job, functools.partial(keep_taps, half)))
 
+    def point_part(part):
+        width = channels // len(one_grad)
+        lanes = slice(part * width, (part + 1) * width)
+        one_grad[part][...] = dot_split(read_pair(ut_pair), (dh_pair[0][:, lanes], dh_pair[1][:, lanes]))
+        job = reduce_all_job(net, one_grad[part], *one_scratch[part], grad_one[part])
+        background.append(then(job, lambda: loads.leave(grad_one[part], one_out.at[:, pl.ds(part * width, width)])))
+
     early = blocks // 2
     for index in range(blocks):
+        block_taps(index)
+        if 1 <= index <= early:
+            block_back(index - 1)
+        if index == early and len(one_grad) == 2:
+            point_part(0)
+        progress()
+    for index in range(early, blocks):
         block_back(index)
-        if 1 <= index <= early:
-            block_taps(index - 1)
         progress()
-    one_grad[...] = dot_split(read_pair(ut_pair), read_pair(dh_pair))
-    job = reduce_all_job(net, one_grad, *one_scratch, grad_one)
-    background.append(then(job, lambda: loads.leave(grad_one, one_out)))
+    point_part(len(one_grad) - 1)
     progress()
 
     def last_sums(index, carry):
@@ -1252,10 +1262,8 @@
     write_sums(sums_own, *lax.fori_loop(0, pixels // TILE, last_sums, (zero, zero)))
     sums = all_sum_job(net, sums_own, total, *sums_slots)
     next(sums)
-    for index in range(early, blocks):
-        block_taps(index)
-        progress()
-        next(sums, None)
+    next(sums)
+    progress()
     finish(sums)
     grad_bias, grad_gain = read_sums(total)
     came_back.wait()
@@ -1329,6 +1337,8 @@
     def pair(*dims):
         return [pltpu.VMEM(dims, BF16)] * 2
 
+    halves = 2 if channels // (dp * rows) % 8 == 0 else 1
+    one_part = [pltpu.VMEM((channels, channels // halves), F32)] * halves
     field = pltpu.VMEM((pixels, channels), F32)
     square = pltpu.VMEM((channels, channels), F32)
     scratch = [
@@ -1357,13 +1367,13 @@
         pair(channels, channels),
         pair(pixels, channels),
         field,
-        square,
-        square,
+        one_part,
+        one_part,
         square,
         square,
         square,
         all_scratch(mesh, channels, channels),
-        all_scratch(mesh, channels, channels),
+        [all_scratch(mesh, channels, channels // halves)] * halves,
         [all_scratch(mesh, tap_rows, 2 * LANES)] * (blocks // 2),
     ]
     smem = pl.BlockSpec(memory_space=pltpu.SMEM)
@@ -1390,7 +1400,8 @@
     up_in,
     down_in,
     point_in,
-    taps_in,
+    big_in,
+    small,
     mask_in,
     params,
     to_freq,
@@ -1409,6 +1420,7 @@
     up,
     down,
     point_one,
+    big,
     taps,
     mask,
     load_sem,
@@ -1435,7 +1447,7 @@
     came_x = loads.start(x_in, x)
     came_point = loads.start(point_in, point_one)
     came_mask = loads.start(mask_in, mask)
-    came_taps = loads.start(taps_in, taps)
+    came_taps = loads.start(big_in, big)
     net.ready()
     sums = all_sum_job(net, value, total, *sums_slots)
     next(sums)
@@ -1471,6 +1483,8 @@
     came_mask.wait()
     finish(sums)
     progress()
+    near = weights_layer_job(net, wall, (1,))
+    next(near)
     mean, inv = norm_terms(total, read_count(total))
 
     def first_norm(index, carry):
@@ -1495,6 +1509,11 @@
         waits += [start_halo(net, act, window, index) for index in (2 * half, 2 * half + 1)]
     loads.leave(hidden, hidden_out)
     came_taps.wait()
+    taps[...] = jnp.zeros(taps.shape, F32)
+    taps[:SPAN, :SPAN, :] = big[...]
+    small_span = small.shape[0]
+    middle_taps = slice(REACH - small_span // 2, REACH + small_span // 2 + 1)
+    taps[middle_taps, middle_taps, :] = big[middle_taps, middle_taps, :] + small[...]
     group = taps_freq.shape[0] // FREQ
     for index in range(blocks):
         for first in range(0, taps.shape[0], group):
@@ -1509,6 +1528,7 @@
     for one in moved:
         one.wait()
     list_rows(rows, name_rows, row_table, tap_table)
+    next(near, None)
     sums = [jnp.zeros((1, LANES), F32)] * 2 * blocks
     for index in range(blocks):
         lanes = slice(index * LANES, (index + 1) * LANES)
@@ -1529,6 +1549,7 @@
     for index in range(blocks):
         conv_sums[index : index + 1, :] = sums[2 * index]
         conv_sums[4 + index : 5 + index, :] = sums[2 * index + 1]
+    finish(near)
     while background:
         progress()
     loads.finish()
@@ -1566,7 +1587,7 @@
     return jnp.concatenate([total[8 + row : 9 + row, :] for row in range(4)], axis=1)
 
 
-def first(mesh, value, names, x, up, down, point_one, taps, mask, params):
+def first(mesh, value, names, x, up, down, point_one, big, small, mask, params):
     dp, devices = mesh
     pixels, channels = x.shape
     lines = pixels // SLOTS
@@ -1586,7 +1607,8 @@
         pltpu.VMEM(up.shape, F32),
         pltpu.VMEM(down.shape, F32),
         pltpu.VMEM(point_one.shape, F32),
-        pltpu.VMEM(taps.shape, F32),
+        pltpu.VMEM(big.shape, F32),
+        pltpu.VMEM((TAP_ROWS, SPAN_PAD, channels), F32),
         pltpu.VMEM(mask.shape, F32),
         pltpu.SemaphoreType.DMA((24,)),
         sum_scratch(mesh, value.shape[0]),
@@ -1609,8 +1631,8 @@
         0,
         mesh,
         first_kernel,
-        (value, names, x, up, down, point_one, taps, mask, params, *constants),
-        [VMEM, VMEM] + [HBM] * 6 + [VMEM] * 4,
+        (value, names, x, up, down, point_one, big, small, mask, params, *constants),
+        [VMEM, VMEM] + [HBM] * 5 + [VMEM, HBM] + [VMEM] * 4,
         [
             shape(pixels, channels),
             shape(devices, 2, *up.shape),
@@ -1627,6 +1649,87 @@
         48,
         late=True,
     )
+
+
+def begin_kernel(place, id_lanes, inputs, grads, x, gy, mask, value):
+    rows = x.shape[0] // SLOTS
+    columns = id_lanes.shape[0] // rows
+    blocks = x.shape[1] // LANES
+
+    def one_row(row, sums):
+        sums = list(sums)
+        for side, (start, width) in enumerate(((0, LEFT), (LEFT, RIGHT))):
+            name, at = place[2 * side, row], place[2 * side + 1, row]
+            pixel = row * columns + at
+            slots = pl.ds(row * SLOTS + start, width)
+            own = jnp.where(name < 0, -9, name).astype(F32)
+            m = jnp.where(id_lanes[pl.ds(pixel, width), :] == own, 1.0, 0.0)
+            mask[slots, :] = m
+            sums[-1] = sums[-1] + column_sum(m)
+            for block in range(blocks):
+                lanes = slice(block * LANES, (block + 1) * LANES)
+                cells = pl.ds(pixel * blocks + block, width, stride=blocks)
+                v = inputs[cells, :] * m
+                x[slots, lanes] = v
+                gy[slots, lanes] = grads[cells, :] * m
+                sums[block] = sums[block] + column_sum(v)
+                sums[blocks + block] = sums[blocks + block] + column_sum(v * v)
+        return tuple(sums)
+
+    sums = lax.fori_loop(0, rows, one_row, (jnp.zeros((1, LANES), F32),) * (2 * blocks + 1))
+    for row in range(2 * blocks):
+        value[row : row + 1, :] = sums[row]
+    for row in range(blocks):
+        value[2 * blocks + row : 2 * blocks + row + 1, :] = sums[-1]
+    value[3 * blocks :, :] = jnp.zeros((value.shape[0] - 3 * blocks, LANES), F32)
+
+
+def begin(place, id_lanes, inputs, grads, rows, channels):
+    return pl.pallas_call(
+        begin_kernel,
+        out_shape=[
+            shape(rows * SLOTS, channels),
+            shape(rows * SLOTS, channels),
+            shape(rows * SLOTS, LANES),
+            shape(16, LANES),
+        ],
+        in_specs=[pl.BlockSpec(memory_space=pltpu.SMEM)] + [VMEM] * 3,
+        out_specs=[VMEM] * 4,
+        compiler_params=pltpu.CompilerParams(vmem_limit_bytes=16 << 20),
+        name="begin",
+    )(place, id_lanes, inputs, grads)
+
+
+def finish_kernel(place, inputs, grads, delta, cells, output, grad_input):
+    rows = delta.shape[0] // SLOTS
+    blocks = delta.shape[1] // LANES
+    columns = inputs.shape[0] // rows // blocks
+    output[...] = inputs[...]
+    grad_input[...] = grads[...]
+
+    def one_row(row, carry):
+        for side, (start, width) in enumerate(((0, LEFT), (LEFT, RIGHT))):
+            pixel = row * columns + place[2 * side + 1, row]
+            slots = pl.ds(row * SLOTS + start, width)
+            for block in range(blocks):
+                lanes = slice(block * LANES, (block + 1) * LANES)
+                where = pl.ds(pixel * blocks + block, width, stride=blocks)
+                output[where, :] = output[where, :] + delta[slots, lanes]
+                grad_input[where, :] = grad_input[where, :] + cells[slots, lanes]
+        return carry
+
+    lax.fori_loop(0, rows, one_row, 0)
+
+
+def place_results(place, inputs, grads, delta, cells):
+    return pl.pallas_call(
+        finish_kernel,
+        out_shape=[shape(*inputs.shape)] * 2,
+        in_specs=[pl.BlockSpec(memory_space=pltpu.SMEM)] + [VMEM] * 4,
+        out_specs=[VMEM] * 2,
+        compiler_params=pltpu.CompilerParams(vmem_limit_bytes=16 << 20),
+        name="finish",
+    )(place, inputs, grads, delta, cells)
 
 
 def shards(
@@ -1665,47 +1768,10 @@
 
     left_id, left_at = side(is_left, LEFT)
     right_id, right_at = side(is_right, RIGHT)
-    slot_column = jnp.concatenate(
-        [
-            left_at[:, None] + jnp.arange(LEFT, dtype=jnp.int32)[None, :],
-            right_at[:, None] + jnp.arange(RIGHT, dtype=jnp.int32)[None, :],
-        ],
-        axis=1,
-    )
-    slot_id = jnp.concatenate(
-        [
-            jnp.broadcast_to(left_id[:, None], (rows, LEFT)),
-            jnp.broadcast_to(right_id[:, None], (rows, RIGHT)),
-        ],
-        axis=1,
-    )
-    hit = (slot_column[:, :, None] == place[:, None, :]) & (ids[:, None, :] == slot_id[:, :, None])
-    hit = hit & (slot_id[:, :, None] >= 0)
-    pick = hit.astype(F32)
-    slot_mask = jnp.max(pick, axis=2)
-    valid = (ids >= 0).astype(F32)
-
-    def compact(field):
-        out = lax.dot_general(
-            pick, field[:, 0], (((2,), (1,)), ((0,), (0,))), precision=HIGHEST, preferred_element_type=F32
-        )
-        return out.reshape(pixels, channels)
-
-    def expand(cells):
-        return lax.dot_general(
-            pick,
-            cells.reshape(rows, SLOTS, channels),
-            (((1,), (1,)), ((0,), (0,))),
-            precision=HIGHEST,
-            preferred_element_type=F32,
-        )[:, None]
-
-    def pack(first, second):
-        return jnp.stack([first, second]).reshape(2 * channels // LANES, LANES)
-
-    def sums(field):
-        return jnp.sum(field, axis=0), jnp.sum(field * field, axis=0)
-
+    spot = jnp.stack([left_id, left_at, right_id, right_at])
+    lines = (rows * columns * channels // LANES, LANES)
+    id_lanes = jnp.broadcast_to(ids.reshape(rows * columns, 1).astype(F32), (rows * columns, LANES))
+    x, gy, mask_lanes, value = begin(spot, id_lanes, inputs.reshape(lines), out_grad.reshape(lines), rows, channels)
     names = jnp.stack([left_id, right_id]) + 1
 
     def name_tile(first, last, lane):
@@ -1718,13 +1784,7 @@
             name_tile(0, REACH, REACH + rows),
         ]
     )
-    x = compact(inputs)
-    gy = compact(out_grad)
-    mask_lanes = jnp.broadcast_to(slot_mask.reshape(pixels, 1), (pixels, LANES))
     small_start = REACH - kernel_small.shape[0] // 2
-    edge = (small_start, small_start)
-    kernel = kernel_big + jnp.pad(kernel_small, (edge, edge, (0, 0)))
-    taps = jnp.pad(kernel, ((0, TAP_ROWS - SPAN), (0, SPAN_PAD - SPAN), (0, 0)))
     vectors = [
         first_norm_gain,
         first_norm_bias,
@@ -1733,21 +1793,22 @@
         feedforward_norm_gain,
         feedforward_norm_bias,
     ]
-    params = jnp.pad(jnp.stack(vectors), ((0, 10), (0, 0)))
+    params = jnp.stack(vectors + [jnp.zeros((channels,), F32)] * 2)
     hidden, wall, xf, kf, conv, conv_sums, total_one, *tables = first(
         mesh,
-        jnp.concatenate([pack(*sums(x)), pack(jnp.full((channels,), jnp.sum(valid)), jnp.zeros((channels,)))]),
+        value,
         names,
         x,
         w_up,
         w_down,
         point_one,
-        taps,
+        kernel_big,
+        kernel_small,
         mask_lanes,
-        params[0:8],
+        params,
     )
     delta, back_three, total_four, total_five, dconv, point_grad, part, _ = middle(
-        mesh, conv, conv_sums, x, gy, mask_lanes, params[2:10], total_one, point_two, wall
+        mesh, conv, conv_sums, x, gy, mask_lanes, params, total_one, point_two, wall
     )
     grad_bias_three, grad_gain_three = total_four.reshape(2, channels)
     grad_bias_two, grad_gain_two = total_five.reshape(2, channels)
@@ -1761,20 +1822,19 @@
         x,
         hidden,
         point_one,
-        params[0:8],
+        params,
         total_one,
         back_three,
         part,
         point_grad,
     )
     grad_bias_one, grad_gain_one = total.reshape(2, channels)
-    output = inputs + expand(delta)
-    grad_input = out_grad + expand(cells)
+    output, grad_input = place_results(spot, inputs.reshape(lines), out_grad.reshape(lines), delta, cells)
     small_end = small_start + kernel_small.shape[0]
     grad_small = grad_kernel[small_start:small_end, small_start:small_end]
     return (
-        output,
-        grad_input,
+        output.reshape(inputs.shape),
+        grad_input.reshape(inputs.shape),
         grad_gain_one,
         grad_bias_one,
         grad_point_one,

time: 307 us -> 288 us (0.938)
  matrix products: 8.79 us -> 0 us
  other arithmetic: 5.41 us -> 1.6 us
    dot_general x4 -> x0, matrix products: 8.79 us -> none  [the longest x2 5.48 us: compact(): lax.dot_general(pick, field[:, 0], (((2,), (1,)), ((0,), (0,))), precisio...]
    pallas_call x3, Pallas kernels: 261 us -> 254 us  [exchange(): pl.pallas_call(kernel, out_shape=outs, in_specs=in_specs, out_specs=out_s...]
    pallas_call x0 -> x2, Pallas kernels: none -> 4.01 us  [the longest x1 2.76 us: place_results(): pl.pallas_call(finish_kernel, out_shape=[shape(*inputs.shape)] * 2, in_sp...]
    unnamed x59 -> x63, local copies, waits for them, and re-layouts: 17.7 us -> 18.9 us
where the time goes in v2:
time: 288 us; the launch traced here: 285 us
  Pallas kernels  258 us (90%)
  local copies, waits for them, and re-layouts  24.1 us (8%)
    pallas_call x3, Pallas kernels, exchange(): pl.pallas_call(kernel, out_shape=outs, in_specs=in_specs, out_specs=out_s...  254 us
    unnamed x63, local copies, waits for them, and re-layouts  18.9 us

profile of v2, /device:TPU:0, one launch (start us, length us, event | category | flops | bytes accessed | tf_op | source)
XLA Modules:
  0.0 284.6 jit_solution(10485143045342505894)
XLA Ops:
  0.6 0.8 select_reduce_fusion.1
  1.5 0.1 fusion.2
  1.6 0.1 pad_bitcast_fusion.2
  1.7 0.1 pad_bitcast_fusion
  1.8 0.7 convert_reduce_fusion
  2.5 0.0 copy-start.17
  2.5 0.1 convert_element_type.12
  2.6 0.8 stack.67.refs_9_.refs_5_
  3.4 0.0 copy-start.15
  3.4 0.0 copy-start.14
  3.4 0.0 copy-start.16
  3.4 0.1 broadcast_in_dim.33.id_lanes
  3.6 0.0 copy-start.1
  3.6 1.4 copy-done.1
  5.0 1.4 copy-done.3
  6.3 1.3 begin.1
  7.6 0.0 copy-start
  7.6 1.0 copy-done
  8.7 1.1 copy-done.10
  9.7 0.0 copy-done.14
  9.7 0.0 copy-done.16
  9.8 58.9 %first.1 = (f32[640,512]{1,0:T(8,128)S(1)}, f32[4,2,512,512]{3,2,1,0:T(8,128)}, f32[4,43,80,128]{3,2,1,0:T(8,128)}, f32[4,28,80,128]{3,2,1,0:T(8,128)}, f32[640,...) custom-call(f32[16,128]{1,0:T(8,128)S(1)} %get-tuple-element.43.refs, ...), custom_call_target="tpu_custom_call" | custom-call | tf_op jit(solution)/shard_map/first/pallas_call | solution.py:436
  68.7 0.0 copy-start.7
  68.7 1.0 copy-done.7
  69.8 0.6 copy-done.18
  70.4 0.6 copy-done.19
  71.0 0.6 copy-done.20
  71.6 0.6 copy-done.21
  72.2 100.5 %middle.1 = (f32[640,512]{1,0:T(8,128)}, f32[640,512]{1,0:T(8,128)}, f32[8,128]{1,0:T(8,128)}, f32[8,128]{1,0:T(8,128)}, f32[16,40,512]{2,1,0:T(8,128)}, /*index...) custom-call(f32[640,512]{1,0:T(8,128)} %get-tuple-element.46.refs_0_, ...), custom_call_target="tpu_custom_call", output_to_operand_aliasing={{7}: (8, {})} | custom-call | tf_op jit(solution)/shard_map/middle/pallas_call | solution.py:436
  172.7 0.0 copy-start.2
  172.7 0.0 copy-start.4
  172.7 94.3 %last.1 = (f32[640,512]{1,0:T(8,128)}, f32[8,128]{1,0:T(8,128)}, f32[512,512]{1,0:T(8,128)}, f32[512,512]{1,0:T(8,128)}, f32[512,512]{1,0:T(8,128)}, /*index=5*/f32[512,512]{1,0:T(8,128)}, f32[27,27,512]{2,1,0:T(8,128)}) custom-call(s32[32,128]{1,0:T(8,128)} %copy-done.19, s32[32,128]{1,0:T(8,128)} %copy-done.20, f32[16,40,512]{2,1,0:T(8,128)} %get-tuple-element.54.refs_2_, ...), custom_call_target="tpu_custom_call" | custom-call | tf_op jit(solution)/shard_map/last/pallas_call | solution.py:436
  267.0 1.3 slice_bitcast_fusion.4
  268.4 0.6 slice_bitcast_fusion.2
  268.9 0.6 slice_bitcast_fusion
  269.5 1.5 slice.17
  271.1 1.3 copy-done.8
  272.4 1.3 copy-done.9
  273.7 2.8 finish.1
  276.5 1.0 copy.46
  277.4 0.9 copy-done.22
  278.3 1.2 copy.47
  279.5 0.7 copy-done.25
  280.2 1.0 copy.48
  281.2 0.6 copy-done.24
  281.8 1.0 copy.49
  282.8 0.6 copy-done.23
  283.4 1.0 copy.50
  (37 shorter events, 0.1 us)
Async XLA Ops:
  2.5 7.2 %copy-start.17 = (f32[5,5,512]{2,1,0:T(8,128)S(1)}, f32[5,5,512]{2,1,0:T(8,128)}, u32[]{:S(2)}) copy-start(f32[5,5,512]{2,1,0:T(8,128)} %refs_7_.2) | copy-start | bytes 153604
  3.4 6.3 %copy-start.15 = (f32[8,512]{1,0:T(8,128)}, f32[8,512]{1,0:T(8,128)S(1)}, u32[]{:S(2)}) copy-start(f32[8,512]{1,0:T(8,128)S(1)} %stack.67.refs_9_.refs_5_) | copy-start | bytes 49156
  3.4 6.3 %copy-start.14 = (bf16[160,240]{1,0:T(8,128)(2,1)S(1)}, bf16[160,240]{1,0:T(8,128)(2,1)}, u32[]{:S(2)}) copy-start(bf16[160,240]{1,0:T(8,128)(2,1)} %constant.13.clone.refs_10_.refs_14_) | copy-start | bytes 230404
  3.4 6.3 %copy-start.16 = (bf16[320,384]{1,0:T(8,128)(2,1)S(1)}, bf16[320,384]{1,0:T(8,128)(2,1)}, u32[]{:S(2)}) copy-start(bf16[320,384]{1,0:T(8,128)(2,1)} %constant.30.clone.refs_11_) | copy-start | bytes 737284
  3.6 1.4 copy-start.1
  5.0 1.4 copy-start.3
  6.3 3.4 %copy-start.5 = (f32[512,512]{1,0:T(8,128)S(1)}, f32[512,512]{1,0:T(8,128)}, u32[]{:S(2)}) copy-start(f32[512,512]{1,0:T(8,128)} %refs_8_.1) | copy-start | bytes 3145732
  6.3 3.4 %copy-start.11 = (f32[512,512]{1,0:T(8,128)S(1)}, f32[512,512]{1,0:T(8,128)}, u32[]{:S(2)}) copy-start(f32[512,512]{1,0:T(8,128)} %refs_3_.1) | copy-start | bytes 3145732
  6.3 3.4 %copy-start.12 = (f32[512,512]{1,0:T(8,128)S(1)}, f32[512,512]{1,0:T(8,128)}, u32[]{:S(2)}) copy-start(f32[512,512]{1,0:T(8,128)} %refs_4_.1) | copy-start | bytes 3145732
  6.3 3.4 %copy-start.13 = (bf16[80,480]{1,0:T(8,128)(2,1)S(1)}, bf16[80,480]{1,0:T(8,128)(2,1)}, u32[]{:S(2)}) copy-start(bf16[80,480]{1,0:T(8,128)(2,1)} %constant.31.clone.refs_12_.refs_15_) | copy-start | bytes 230404
  7.6 1.1 copy-start
  8.7 1.1 copy-start.10
  9.7 59.0 %copy-start.6 = (f32[640,128]{1,0:T(8,128)}, f32[640,128]{1,0:T(8,128)S(1)}, u32[]{:S(2)}) copy-start(f32[640,128]{1,0:T(8,128)S(1)} %get-tuple-element.45.refs_8_.refs_4_.refs_5_) | copy-start | bytes 983044
  68.7 1.1 copy-start.7
  69.8 0.6 copy-start.18
  70.4 0.6 copy-start.19
  71.0 0.6 copy-start.20
  71.6 0.6 copy-start.21
  172.7 95.7 %copy-start.28 = (f32[8,128]{1,0:T(8,128)S(1)}, f32[8,128]{1,0:T(8,128)}, u32[]{:S(2)}) copy-start(f32[8,128]{1,0:T(8,128)} %get-tuple-element.67) | copy-start | bytes 12292
  172.7 96.3 %copy-start.27 = (f32[8,128]{1,0:T(8,128)S(1)}, f32[8,128]{1,0:T(8,128)}, u32[]{:S(2)}) copy-start(f32[8,128]{1,0:T(8,128)} %get-tuple-element.69) | copy-start | bytes 12292
  172.7 98.4 %copy-start.2 = (f32[16,1,44,512]{3,1,2,0:T(1,128)S(1)}, f32[16,1,44,512]{3,1,2,0:T(1,128)}, u32[]{:S(2)}) copy-start(f32[16,1,44,512]{3,1,2,0:T(1,128)} %param.21) | copy-start | bytes 4325380
  172.7 98.4 %copy-start.4 = (f32[16,1,44,512]{3,1,2,0:T(1,128)S(1)}, f32[16,1,44,512]{3,1,2,0:T(1,128)}, u32[]{:S(2)}) copy-start(f32[16,1,44,512]{3,1,2,0:T(1,128)} %param.35) | copy-start | bytes 4325380
  271.1 1.3 copy-start.8
  272.4 1.3 copy-start.9
  273.7 2.8 copy-start.26
  276.5 1.9 copy-start.22
  278.3 1.9 copy-start.25
  280.2 1.6 copy-start.24
  281.8 1.6 copy-start.23

commit v3 on v2

--- a/solution.py
+++ b/solution.py
@@ -236,21 +236,22 @@
     ]
 
 
-def weights_line_job(net, up, down, wall):
-    own = [net.own(up, wall.at[net.z, 0]), net.own(down, wall.at[net.z, 1])]
+def weights_line_job(net, up, down, wall, distances):
+    own = [net.own(up, wall.at[net.z, 0]), net.own(down, wall.at[net.z, 1])] if 1 in distances else []
     last = net.rows - 1
-    for step in range(1, net.rows):
+    for step in distances:
         moves = []
-        for lanes, _, base, rows in sides(net, up.shape[0]):
+        for lanes, _, base, rows in sides(net, wall.shape[2]):
             mine = pl.ds(aligned(base, 8), rows)
             for way in (1, -1):
                 shard = net.z - way * (step - 1)
                 going = (net.z >= step - 1) & (net.z < last) if way > 0 else (net.z <= last - (step - 1)) & (net.z > 0)
                 coming = net.z >= step if way > 0 else net.z <= last - step
                 shard = lax.rem(shard + net.rows, net.rows)
-                for which, ref in enumerate((up, down)):
+                for which in range(2):
                     piece = wall.at[shard, which, mine, lanes]
-                    one = net.copy(ref.at[mine, lanes] if step == 1 else piece, piece, net.line(way % net.rows))
+                    source = (up, down)[which].at[mine, lanes] if step == 1 else piece
+                    one = net.copy(source, piece, net.line(way % net.rows))
                     pl.when(going)(one.start)
                     moves.append((one, going, coming))
         if step == 1:
@@ -639,12 +640,10 @@
     job = total_job(0, sums_slots[1].at[0])
     next(job)
 
-    def weights_job():
-        yield from weights_layer_job(net, wall, range(2, net.rows))
-        yield from weights_pair_job(net, wall)
-
-    weights = weights_job()
-    next(weights)
+    far_line = weights_line_job(net, None, None, wall, (net.rows - 1,))
+    next(far_line)
+    near = weights_layer_job(net, wall, range(2, net.rows - 1))
+    next(near, None)
     for one in load(0):
         one.start()
     came_point.wait()
@@ -654,6 +653,7 @@
     next(job)
     store_split(gt_pair, Ellipsis, gy[...].T)
     finish(job)
+    next(near, None)
     for one in came:
         one.wait()
     mean, inv_two = norm_terms(sums_slots[1].at[0], count)
@@ -672,9 +672,13 @@
     write_sums(sums_own.at[1], *each_tile(second_norm))
     job = total_job(1, sums_slots[1].at[1])
     next(job)
-    next(weights)
+    finish(far_line)
+    far = weights_layer_job(net, wall, (net.rows - 1,))
+    next(far)
     next(job)
     finish(job)
+    finish(near)
+    next(far)
     mean_three, inv_three = norm_terms(sums_slots[1].at[1], count)
 
     def third_norm(rows, carry):
@@ -830,10 +834,11 @@
         return carry
 
     lax.fori_loop(0, per_shard - 1, feed_forward, 0)
-    for _ in range(stages - 1):
-        next(weights)
+    finish(far)
+    pairs = weights_pair_job(net, wall)
+    next(pairs)
     lax.fori_loop(per_shard - 1, per_shard, feed_forward, 0)
-    finish(weights)
+    finish(pairs)
     for one in load(per_shard):
         one.start()
     lax.fori_loop(per_shard, chunks, feed_forward, 0)
@@ -851,10 +856,8 @@
     next(job)
     progress(chunks)
     next(job)
+    finish(job)
     progress(chunks + 1)
-    finish(job)
-    for step in range(chunks + 2, chunks + 1 + stages):
-        progress(step)
     grad_bias, grad_gain = read_sums(total_four)
 
     def third_back(rows, carry):
@@ -872,6 +875,8 @@
     loads.leave(back, back_out)
     job = total_job(3, total_five)
     next(job)
+    for step in range(chunks + 2, chunks + 1 + stages):
+        progress(step)
     for side in range(2):
         ut_pair[side][...] = act_pair[side][...].T
     next(job)
@@ -1016,7 +1021,7 @@
                 for row in range(rows):
                     dr, di = d_ref[REACH + row, real, :], d_ref[REACH + row, imag, :]
                     for k in range(TAP_GROUP):
-                        w = table[side * rows + row, group * TAP_GROUP + k]
+                        w = table[side * SPAN + group * TAP_GROUP + k, row]
                         xr, xi = x_ref[w, real, :], x_ref[w, imag, :]
                         gr, gi = sums[k]
                         sums[k] = gr + (dr * xr + di * xi), gi + (dr * xi - di * xr)
@@ -1470,7 +1475,7 @@
     came_up.wait()
     came_down.wait()
 
-    background = [weights_line_job(net, up, down, wall)]
+    background = [weights_line_job(net, up, down, wall, range(1, net.rows - 1))]
 
     def progress():
         background[:] = [job for job in background if next(job, StopIteration) is not StopIteration]
@@ -1482,9 +1487,6 @@
     came_x.wait()
     came_mask.wait()
     finish(sums)
-    progress()
-    near = weights_layer_job(net, wall, (1,))
-    next(near)
     mean, inv = norm_terms(total, read_count(total))
 
     def first_norm(index, carry):
@@ -1507,6 +1509,9 @@
                 TILE // SLOTS, SLOTS, 2 * LANES
             )
         waits += [start_halo(net, act, window, index) for index in (2 * half, 2 * half + 1)]
+    progress()
+    near = weights_layer_job(net, wall, (1,))
+    next(near)
     loads.leave(hidden, hidden_out)
     came_taps.wait()
     taps[...] = jnp.zeros(taps.shape, F32)
@@ -1543,8 +1548,6 @@
             conv[where, lanes] = cells
             sums[2 * index] = sums[2 * index] + column_sum(cells)
             sums[2 * index + 1] = sums[2 * index + 1] + column_sum(cells * cells)
-        if index == 0:
-            progress()
     loads.leave(conv, conv_out)
     for index in range(blocks):
         conv_sums[index : index + 1, :] = sums[2 * index]
@@ -1577,7 +1580,7 @@
                 row_table[side * rows + row, tap] = jnp.where(low + tap < high, low + tap, ZERO_ROW)
             for tap in range(SPAN):
                 w = row + tap
-                tap_table[side * rows + row, tap] = jnp.where((w >= low) & (w < high), w, ZERO_ROW)
+                tap_table[side * SPAN + tap, row] = jnp.where((w >= low) & (w < high), w, ZERO_ROW)
             return carry
 
         lax.fori_loop(0, rows, one_row, 0)
@@ -1625,7 +1628,6 @@
         field,
     ]
     smem = pl.BlockSpec(memory_space=pltpu.SMEM)
-    table = jax.ShapeDtypeStruct((2 * lines, LANES), jnp.int32)
     return exchange(
         "first",
         0,
@@ -1641,12 +1643,12 @@
             shape(pixels, channels),
             shape(8, LANES),
             shape(*value.shape),
-            table,
-            table,
+            jax.ShapeDtypeStruct((2 * lines, LANES), jnp.int32),
+            jax.ShapeDtypeStruct((2 * SPAN, LANES), jnp.int32),
         ],
         [HBM] * 5 + [VMEM] * 2 + [smem] * 2,
         scratch,
-        48,
+        60,
         late=True,
     )
 
@@ -1727,7 +1729,7 @@
         out_shape=[shape(*inputs.shape)] * 2,
         in_specs=[pl.BlockSpec(memory_space=pltpu.SMEM)] + [VMEM] * 4,
         out_specs=[VMEM] * 2,
-        compiler_params=pltpu.CompilerParams(vmem_limit_bytes=16 << 20),
+        compiler_params=pltpu.CompilerParams(vmem_limit_bytes=60 << 20),
         name="finish",
     )(place, inputs, grads, delta, cells)
 

time: 288 us -> 277 us (0.962)
  Pallas kernels: 258 us -> 249 us
  local copies, waits for them, and re-layouts: 24.1 us -> 19.9 us
    pallas_call x3, Pallas kernels: 254 us -> 243 us  [exchange(): pl.pallas_call(kernel, out_shape=outs, in_specs=in_specs, out_specs=out_s...]
    unnamed x63 -> x33, local copies, waits for them, and re-layouts: 18.9 us -> 14.1 us
where the time goes in v3:
time: 277 us; the launch traced here: 272 us
  Pallas kernels  249 us (90%)
  local copies, waits for them, and re-layouts  19.9 us (7%)
    pallas_call x3, Pallas kernels, exchange(): pl.pallas_call(kernel, out_shape=outs, in_specs=in_specs, out_specs=out_s...  243 us
    unnamed x33, local copies, waits for them, and re-layouts  14.1 us

profile of v3, /device:TPU:0, one launch (start us, length us, event | category | flops | bytes accessed | tf_op | source)
XLA Modules:
  0.0 272.5 jit_solution(7327716437727651281)
XLA Ops:
  0.6 0.8 select_reduce_fusion.1
  1.5 0.0 copy-start.5
  1.6 0.1 fusion.2
  1.6 0.1 pad_bitcast_fusion.2
  1.7 0.1 pad_bitcast_fusion
  1.8 0.6 pad_add_fusion.refs_1_
  2.4 0.7 convert_reduce_fusion
  3.1 0.1 convert_element_type.12
  3.2 1.4 stack.67.refs_9_.refs_5_
  4.6 0.1 broadcast_in_dim.33.id_lanes
  4.7 0.0 copy-start.1
  4.8 1.4 copy-done.1
  6.1 0.0 copy-start.2
  6.1 1.4 copy-done.2
  7.5 1.2 begin.1
  8.7 0.0 copy-done.5
  8.7 0.0 copy-start
  8.8 1.0 copy-done
  9.8 0.0 copy-start.3
  9.8 0.7 copy-done.3
  10.5 0.0 copy-start.4
  10.5 1.1 copy-done.4
  11.6 0.0 copy-start.6
  11.6 0.6 copy-done.6
  12.2 54.3 %first.1 = (f32[640,512]{1,0:T(8,128)}, f32[4,2,512,512]{3,2,1,0:T(8,128)}, f32[4,43,80,128]{3,2,1,0:T(8,128)}, f32[4,28,80,128]{3,2,1,0:T(8,128)}, f32[640,512]...) custom-call(f32[16,128]{1,0:T(8,128)} %copy-done.6, ...), custom_call_target="tpu_custom_call" | custom-call | tf_op jit(solution)/shard_map/first/pallas_call | solution.py:437
  66.5 95.7 %middle.1 = (f32[640,512]{1,0:T(8,128)}, f32[640,512]{1,0:T(8,128)}, f32[8,128]{1,0:T(8,128)}, f32[8,128]{1,0:T(8,128)}, f32[16,40,512]{2,1,0:T(8,128)}, /*index...) custom-call(f32[640,512]{1,0:T(8,128)} %get-tuple-element.46.refs_0_, ...), custom_call_target="tpu_custom_call", output_to_operand_aliasing={{7}: (8, {})} | custom-call | tf_op jit(solution)/shard_map/middle/pallas_call | solution.py:437
  162.1 0.0 copy-start.13
  162.2 0.0 copy-start.12
  162.2 93.3 %last.1 = (f32[640,512]{1,0:T(8,128)}, f32[8,128]{1,0:T(8,128)}, f32[512,512]{1,0:T(8,128)}, f32[512,512]{1,0:T(8,128)}, f32[512,512]{1,0:T(8,128)}, /*index=5*/f32[512,512]{1,0:T(8,128)}, f32[27,27,512]{2,1,0:T(8,128)}) custom-call(s32[32,128]{1,0:T(8,128)} %get-tuple-element.52.refs_0_, s32[54,128]{1,0:T(8,128)} %get-tuple-element.53.refs_1_, ...), custom_call_target="tpu_custom_call" | custom-call | tf_op jit(solution)/shard_map/last/pallas_call | solution.py:437
  255.5 1.3 slice_bitcast_fusion.4
  256.8 0.0 copy-done.13
  256.8 0.6 slice_bitcast_fusion.2
  257.4 0.0 copy-done.12
  257.4 0.6 slice_bitcast_fusion
  258.0 1.5 slice.17
  259.5 0.0 copy-start.11
  259.5 4.9 %finish.1 = (f32[2816,128]{1,0:T(8,128)}, f32[2816,128]{1,0:T(8,128)}) custom-call(s32[4,16]{1,0:T(4,128)} %copy-done.5, f32[2816,128]{1,0:T(8,128)} %bitcast.35, f32[2816,128]{1,0:T(8,128)} %bitcast.37, f32[640,512]{1,0:T(8,128)} %get-tuple-element.51.delta, f32[640,512]{1,0:T(8,128)} %get-tuple-element.61.cells), custom_call_target="tpu_custom_call" | custom-call | tf_op jit(solution)/shard_map/finish/pallas_call | solution.py:1727
  264.4 0.0 copy-start.7
  264.4 0.0 copy-done.11
  264.4 1.0 copy.46
  265.4 0.9 copy-done.7
  266.3 1.2 copy.47
  267.5 0.7 copy-done.10
  268.1 1.0 copy.48
  269.1 0.6 copy-done.9
  269.7 1.0 copy.49
  270.7 0.6 copy-done.8
  271.3 1.0 copy.50
  (7 shorter events, 0.0 us)
Async XLA Ops:
  1.5 7.2 %copy-start.5 = (s32[4,16]{1,0:T(4,128)}, s32[4,16]{1,0:T(4,128)S(1)}, u32[]{:S(2)}) copy-start(s32[4,16]{1,0:T(4,128)S(1)} %pad_add_fusion.1.place) | copy-start | bytes 772
  4.7 1.4 copy-start.1
  6.1 1.4 copy-start.2
  8.7 1.1 copy-start
  9.8 0.7 copy-start.3
  10.5 1.1 copy-start.4
  11.6 0.6 copy-start.6
  162.1 94.7 %copy-start.13 = (f32[8,128]{1,0:T(8,128)S(1)}, f32[8,128]{1,0:T(8,128)}, u32[]{:S(2)}) copy-start(f32[8,128]{1,0:T(8,128)} %get-tuple-element.67) | copy-start | bytes 12292
  162.2 95.2 %copy-start.12 = (f32[8,128]{1,0:T(8,128)S(1)}, f32[8,128]{1,0:T(8,128)}, u32[]{:S(2)}) copy-start(f32[8,128]{1,0:T(8,128)} %get-tuple-element.69) | copy-start | bytes 12292
  259.5 4.9 %copy-start.11 = (f32[512,512]{1,0:T(8,128)S(1)}, f32[512,512]{1,0:T(8,128)}, u32[]{:S(2)}) copy-start(f32[512,512]{1,0:T(8,128)} %get-tuple-element.134) | copy-start | bytes 3145732
  264.4 1.9 copy-start.7
  266.3 1.9 copy-start.10
  268.1 1.6 copy-start.9
  269.7 1.6 copy-start.8

commit v4 on v3

--- a/solution.py
+++ b/solution.py
@@ -1702,36 +1702,92 @@
     )(place, id_lanes, inputs, grads)
 
 
-def finish_kernel(place, inputs, grads, delta, cells, output, grad_input):
+def finish_kernel(
+    place,
+    inputs,
+    grads,
+    delta_in,
+    cells_in,
+    one_in,
+    two_in,
+    up_in,
+    down_in,
+    cube_in,
+    total_three,
+    total_two,
+    total_one,
+    output,
+    grad_input,
+    one_out,
+    two_out,
+    up_out,
+    down_out,
+    cube_out,
+    small,
+    *rest,
+):
+    vectors, (field, field_back, delta, cells, squares, cube, sems) = rest[:6], rest[6:]
     rows = delta.shape[0] // SLOTS
     blocks = delta.shape[1] // LANES
-    columns = inputs.shape[0] // rows // blocks
-    output[...] = inputs[...]
-    grad_input[...] = grads[...]
-
-    def one_row(row, carry):
-        for side, (start, width) in enumerate(((0, LEFT), (LEFT, RIGHT))):
-            pixel = row * columns + place[2 * side + 1, row]
-            slots = pl.ds(row * SLOTS + start, width)
-            for block in range(blocks):
-                lanes = slice(block * LANES, (block + 1) * LANES)
-                where = pl.ds(pixel * blocks + block, width, stride=blocks)
-                output[where, :] = output[where, :] + delta[slots, lanes]
-                grad_input[where, :] = grad_input[where, :] + cells[slots, lanes]
-        return carry
-
-    lax.fori_loop(0, rows, one_row, 0)
-
-
-def place_results(place, inputs, grads, delta, cells):
+    columns = field.shape[0] // rows // blocks
+    loads = Loads(sems)
+    came = [[loads.start(inputs, field), loads.start(delta_in, delta)], [loads.start(grads, field_back), loads.start(cells_in, cells)]]
+    through = [
+        (loads.start(src, middle), middle, out)
+        for src, middle, out in zip(
+            (one_in, two_in, up_in, down_in, cube_in), (*squares, cube), (one_out, two_out, up_out, down_out, cube_out)
+        )
+    ]
+    for copies, whole, part, out in zip(came, (field, field_back), (delta, cells), (output, grad_input)):
+        for one in copies:
+            one.wait()
+
+        def one_row(row, carry):
+            for side, (start, width) in enumerate(((0, LEFT), (LEFT, RIGHT))):
+                pixel = row * columns + place[2 * side + 1, row]
+                slots = pl.ds(row * SLOTS + start, width)
+                for block in range(blocks):
+                    where = pl.ds(pixel * blocks + block, width, stride=blocks)
+                    whole[where, :] = whole[where, :] + part[slots, block * LANES : (block + 1) * LANES]
+            return carry
+
+        lax.fori_loop(0, rows, one_row, 0)
+        loads.leave(whole, out)
+    for one, middle, out in through:
+        one.wait()
+        loads.leave(middle, out)
+    first = REACH - small.shape[0] // 2
+    last = first + small.shape[0]
+    small[...] = cube[first:last, first:last, :]
+    for which, total in enumerate((total_one, total_two, total_three)):
+        for out, value in zip(vectors[2 * which : 2 * which + 2], read_sums(total)):
+            out[...] = value
+    loads.finish()
+
+
+def place_results(place, inputs, grads, delta, cells, squares, cube, totals, small_span):
+    channels = delta.shape[1]
+    square = pltpu.VMEM((channels, channels), F32)
     return pl.pallas_call(
         finish_kernel,
-        out_shape=[shape(*inputs.shape)] * 2,
-        in_specs=[pl.BlockSpec(memory_space=pltpu.SMEM)] + [VMEM] * 4,
-        out_specs=[VMEM] * 2,
+        out_shape=[shape(*inputs.shape)] * 2
+        + [shape(channels, channels)] * 4
+        + [shape(*cube.shape), shape(small_span, small_span, channels)]
+        + [shape(1, channels)] * 6,
+        in_specs=[pl.BlockSpec(memory_space=pltpu.SMEM)] + [HBM] * 9 + [VMEM] * 3,
+        out_specs=[HBM] * 7 + [VMEM] * 7,
+        scratch_shapes=[
+            pltpu.VMEM(inputs.shape, F32),
+            pltpu.VMEM(inputs.shape, F32),
+            pltpu.VMEM(delta.shape, F32),
+            pltpu.VMEM(delta.shape, F32),
+            [square] * 4,
+            pltpu.VMEM(cube.shape, F32),
+            pltpu.SemaphoreType.DMA((16,)),
+        ],
         compiler_params=pltpu.CompilerParams(vmem_limit_bytes=60 << 20),
         name="finish",
-    )(place, inputs, grads, delta, cells)
+    )(place, inputs, grads, delta, cells, *squares, cube, *totals)
 
 
 def shards(
@@ -1786,7 +1842,6 @@
             name_tile(0, REACH, REACH + rows),
         ]
     )
-    small_start = REACH - kernel_small.shape[0] // 2
     vectors = [
         first_norm_gain,
         first_norm_bias,
@@ -1812,8 +1867,6 @@
     delta, back_three, total_four, total_five, dconv, point_grad, part, _ = middle(
         mesh, conv, conv_sums, x, gy, mask_lanes, params, total_one, point_two, wall
     )
-    grad_bias_three, grad_gain_three = total_four.reshape(2, channels)
-    grad_bias_two, grad_gain_two = total_five.reshape(2, channels)
     cells, total, grad_point_one, grad_point_two, grad_up, grad_down, grad_kernel = last(
         mesh,
         tables,
@@ -1830,10 +1883,20 @@
         part,
         point_grad,
     )
-    grad_bias_one, grad_gain_one = total.reshape(2, channels)
-    output, grad_input = place_results(spot, inputs.reshape(lines), out_grad.reshape(lines), delta, cells)
-    small_end = small_start + kernel_small.shape[0]
-    grad_small = grad_kernel[small_start:small_end, small_start:small_end]
+    squares = (grad_point_one, grad_point_two, grad_up, grad_down)
+    output, grad_input, grad_point_one, grad_point_two, grad_up, grad_down, grad_kernel, grad_small, *vectors = place_results(
+        spot,
+        inputs.reshape(lines),
+        out_grad.reshape(lines),
+        delta,
+        cells,
+        squares,
+        grad_kernel,
+        (total_four, total_five, total),
+        kernel_small.shape[0],
+    )
+    vectors = [vector.reshape(channels) for vector in vectors]
+    grad_bias_one, grad_gain_one, grad_bias_two, grad_gain_two, grad_bias_three, grad_gain_three = vectors
     return (
         output.reshape(inputs.shape),
         grad_input.reshape(inputs.shape),

time: 277 us -> 269 us (0.971)
  local copies, waits for them, and re-layouts: 19.9 us -> 7.99 us
  Pallas kernels: 249 us -> 254 us
    unnamed x33 -> x14, local copies, waits for them, and re-layouts: 14.1 us -> 6.15 us
    pallas_call x1, Pallas kernels: 4.88 us -> 9.33 us  [place_results(): pl.pallas_call(finish_kernel, out_shape=[shape(*inputs.shape)] * 2 + [sha...]
where the time goes in v4:
time: 269 us; the launch traced here: 265 us
  Pallas kernels  254 us (94%)
  local copies, waits for them, and re-layouts  7.99 us (3%)
    pallas_call x3, Pallas kernels, exchange(): pl.pallas_call(kernel, out_shape=outs, in_specs=in_specs, out_specs=out_s...  243 us
    pallas_call x1, Pallas kernels, place_results(): pl.pallas_call(finish_kernel, out_shape=[shape(*inputs.shape)] * 2 + [sha...  9.33 us
    unnamed x14, local copies, waits for them, and re-layouts  6.15 us

profile of v4, /device:TPU:0, one launch (start us, length us, event | category | flops | bytes accessed | tf_op | source)
XLA Modules:
  0.0 265.2 jit_solution(5462104956829012130)
XLA Ops:
  0.6 0.8 select_reduce_fusion.1
  1.5 0.0 copy-start.5
  1.6 0.1 fusion.2
  1.6 0.1 pad_bitcast_fusion.2
  1.7 0.1 pad_bitcast_fusion
  1.8 0.6 pad_add_fusion.refs_1_
  2.4 0.7 convert_reduce_fusion
  3.1 0.1 convert_element_type.12
  3.2 1.4 stack.67.refs_9_.refs_5_
  4.6 0.1 broadcast_in_dim.33.id_lanes
  4.7 0.0 copy-start.1
  4.8 1.4 copy-done.1
  6.1 0.0 copy-start.2
  6.1 1.4 copy-done.2
  7.5 1.2 begin.1
  8.7 0.0 copy-done.5
  8.7 0.0 copy-start
  8.8 1.0 copy-done
  9.8 0.0 copy-start.3
  9.8 0.7 copy-done.3
  10.5 0.0 copy-start.4
  10.5 1.1 copy-done.4
  11.6 0.0 copy-start.6
  11.6 0.6 copy-done.6
  12.2 54.3 %first.1 = (f32[640,512]{1,0:T(8,128)}, f32[4,2,512,512]{3,2,1,0:T(8,128)}, f32[4,43,80,128]{3,2,1,0:T(8,128)}, f32[4,28,80,128]{3,2,1,0:T(8,128)}, f32[640,512]...) custom-call(f32[16,128]{1,0:T(8,128)} %copy-done.6, ...), custom_call_target="tpu_custom_call" | custom-call | tf_op jit(solution)/shard_map/first/pallas_call | solution.py:437
  66.5 95.6 %middle.1 = (f32[640,512]{1,0:T(8,128)}, f32[640,512]{1,0:T(8,128)}, f32[8,128]{1,0:T(8,128)}, f32[8,128]{1,0:T(8,128)}, f32[16,40,512]{2,1,0:T(8,128)}, /*index...) custom-call(f32[640,512]{1,0:T(8,128)} %get-tuple-element.58.refs_0_, ...), custom_call_target="tpu_custom_call", output_to_operand_aliasing={{7}: (8, {})} | custom-call | tf_op jit(solution)/shard_map/middle/pallas_call | solution.py:437
  162.1 93.6 %last.1 = (f32[640,512]{1,0:T(8,128)}, f32[8,128]{1,0:T(8,128)}, f32[512,512]{1,0:T(8,128)}, f32[512,512]{1,0:T(8,128)}, f32[512,512]{1,0:T(8,128)}, /*index=5*/f32[512,512]{1,0:T(8,128)}, f32[27,27,512]{2,1,0:T(8,128)}) custom-call(s32[32,128]{1,0:T(8,128)} %get-tuple-element.64.refs_0_, s32[54,128]{1,0:T(8,128)} %get-tuple-element.65.refs_1_, ...), custom_call_target="tpu_custom_call" | custom-call | tf_op jit(solution)/shard_map/last/pallas_call | solution.py:437
  255.7 9.3 %finish.1 = (f32[2816,128]{1,0:T(8,128)}, f32[2816,128]{1,0:T(8,128)}, f32[512,512]{1,0:T(8,128)}, f32[512,512]{1,0:T(8,128)}, f32[512,512]{1,0:T(8,128)}, /*ind...) custom-call(s32[4,16]{1,0:T(4,128)} %copy-done.5, ...), custom_call_target="tpu_custom_call" | custom-call | tf_op jit(solution)/shard_map/finish/pallas_call | solution.py:1771
  (4 shorter events, 0.0 us)
Async XLA Ops:
  1.5 7.2 %copy-start.5 = (s32[4,16]{1,0:T(4,128)}, s32[4,16]{1,0:T(4,128)S(1)}, u32[]{:S(2)}) copy-start(s32[4,16]{1,0:T(4,128)S(1)} %pad_add_fusion.1.place) | copy-start | bytes 772
  4.7 1.4 copy-start.1
  6.1 1.4 copy-start.2
  8.7 1.1 copy-start
  9.8 0.7 copy-start.3
  10.5 1.1 copy-start.4
  11.6 0.6 copy-start.6

commit v5 on v4

--- a/solution.py
+++ b/solution.py
@@ -335,6 +335,17 @@
     return out
 
 
+def corners(net, steps):
+    (first, base, size), (second, _, _) = steps
+    one, two = net.bit(first), net.bit(second)
+    found = []
+    for turn_one, turn_two in ((1, 0), (0, 1), (1, 1)):
+        step_one, step_two = turn_one * (1 - 2 * one), turn_two * (1 - 2 * two)
+        place = base + (one + step_one) * (size // 2) + (two + step_two) * (size // 4)
+        found.append((place, (net.dp + (1 << first) * step_one + (1 << second) * step_two, net.z)))
+    return found
+
+
 def reduce_all_job(net, source, acc, got_pair, got, got_line, out):
     rows, width = source.shape
     half = width // 2
@@ -348,7 +359,26 @@
     sent.wait()
     add_rows(lambda at: acc.at[pl.ds(at, 64)], lambda at: got_pair.at[pl.ds(at, 64)], rows, 64)
     parts = shares(net, rows, width)
-    for index in range(len(net.bits)):
+    direct = len(net.bits) == 2
+    if direct:
+        moves = []
+        for side, (inner, _, steps, _, size) in enumerate(parts):
+            for slot, (base, device) in enumerate(corners(net, steps)):
+                place = got.at[side, pl.ds(slot * size, size)]
+                moves.append(net.copy(acc.at[pl.ds(aligned(base, 8), size), inner], place, device))
+                moves[-1].start()
+        yield
+        for one in moves:
+            one.wait()
+        for side, (inner, _, _, base, size) in enumerate(parts):
+            for slot in range(3):
+                add_rows(
+                    lambda at: acc.at[pl.ds(aligned(base + at, 8), 8), inner],
+                    lambda at: got.at[side, pl.ds(aligned(slot * size + at, 8), 8)],
+                    size,
+                    8,
+                )
+    for index in range(0 if direct else len(net.bits)):
         moves = []
         for side, (inner, _, steps, _, _) in enumerate(parts):
             bit, base, size = steps[index]
@@ -396,7 +426,17 @@
     yield
     for one in moves:
         one.wait()
-    for back in range(1, len(net.bits) + 1):
+    if direct:
+        moves = []
+        for _, outer, steps, base, size in parts:
+            piece = out.at[pl.ds(aligned(base, 8), size), outer]
+            for _, device in corners(net, steps):
+                moves.append(net.copy(piece, piece, device))
+                moves[-1].start()
+        yield
+        for one in moves:
+            one.wait()
+    for back in range(1, 1 if direct else len(net.bits) + 1):
         moves = []
         for _, outer, steps, _, _ in parts:
             bit, base, size = steps[-back]

time: 269 us -> 275 us (1.022)
  Pallas kernels: 254 us -> 259 us
    pallas_call x3, Pallas kernels: 243 us -> 249 us  [exchange(): pl.pallas_call(kernel, out_shape=outs, in_specs=in_specs, out_specs=out_s...]
where the time goes in v5:
time: 275 us; the launch traced here: 270 us
  Pallas kernels  259 us (94%)
  local copies, waits for them, and re-layouts  7.99 us (3%)
    pallas_call x3, Pallas kernels, exchange(): pl.pallas_call(kernel, out_shape=outs, in_specs=in_specs, out_specs=out_s...  249 us
    pallas_call x1, Pallas kernels, place_results(): pl.pallas_call(finish_kernel, out_shape=[shape(*inputs.shape)] * 2 + [sha...  9.33 us
    unnamed x14, local copies, waits for them, and re-layouts  6.15 us

profile of v5, /device:TPU:0, one launch (start us, length us, event | category | flops | bytes accessed | tf_op | source)
XLA Modules:
  0.0 270.4 jit_solution(5265153008448833675)
XLA Ops:
  0.6 0.8 select_reduce_fusion.1
  1.5 0.0 copy-start.5
  1.6 0.1 fusion.2
  1.6 0.1 pad_bitcast_fusion.2
  1.7 0.1 pad_bitcast_fusion
  1.8 0.6 pad_add_fusion.refs_1_
  2.4 0.7 convert_reduce_fusion
  3.1 0.1 convert_element_type.12
  3.2 1.4 stack.67.refs_9_.refs_5_
  4.6 0.1 broadcast_in_dim.33.id_lanes
  4.7 0.0 copy-start.1
  4.8 1.4 copy-done.1
  6.1 0.0 copy-start.2
  6.1 1.4 copy-done.2
  7.5 1.2 begin.1
  8.7 0.0 copy-done.5
  8.7 0.0 copy-start
  8.8 1.0 copy-done
  9.8 0.0 copy-start.3
  9.8 0.7 copy-done.3
  10.5 0.0 copy-start.4
  10.5 1.1 copy-done.4
  11.6 0.0 copy-start.6
  11.6 0.6 copy-done.6
  12.2 54.3 %first.1 = (f32[640,512]{1,0:T(8,128)}, f32[4,2,512,512]{3,2,1,0:T(8,128)}, f32[4,43,80,128]{3,2,1,0:T(8,128)}, f32[4,28,80,128]{3,2,1,0:T(8,128)}, f32[640,512]...) custom-call(f32[16,128]{1,0:T(8,128)} %copy-done.6, ...), custom_call_target="tpu_custom_call" | custom-call | tf_op jit(solution)/shard_map/first/pallas_call | solution.py:477
  66.5 95.6 %middle.1 = (f32[640,512]{1,0:T(8,128)}, f32[640,512]{1,0:T(8,128)}, f32[8,128]{1,0:T(8,128)}, f32[8,128]{1,0:T(8,128)}, f32[16,40,512]{2,1,0:T(8,128)}, /*index...) custom-call(f32[640,512]{1,0:T(8,128)} %get-tuple-element.58.refs_0_, ...), custom_call_target="tpu_custom_call", output_to_operand_aliasing={{7}: (8, {})} | custom-call | tf_op jit(solution)/shard_map/middle/pallas_call | solution.py:477
  162.1 98.8 %last.1 = (f32[640,512]{1,0:T(8,128)}, f32[8,128]{1,0:T(8,128)}, f32[512,512]{1,0:T(8,128)}, f32[512,512]{1,0:T(8,128)}, f32[512,512]{1,0:T(8,128)}, /*index=5*/f32[512,512]{1,0:T(8,128)}, f32[27,27,512]{2,1,0:T(8,128)}) custom-call(s32[32,128]{1,0:T(8,128)} %get-tuple-element.64.refs_0_, s32[54,128]{1,0:T(8,128)} %get-tuple-element.65.refs_1_, ...), custom_call_target="tpu_custom_call" | custom-call | tf_op jit(solution)/shard_map/last/pallas_call | solution.py:477
  260.9 9.3 %finish.1 = (f32[2816,128]{1,0:T(8,128)}, f32[2816,128]{1,0:T(8,128)}, f32[512,512]{1,0:T(8,128)}, f32[512,512]{1,0:T(8,128)}, f32[512,512]{1,0:T(8,128)}, /*ind...) custom-call(s32[4,16]{1,0:T(4,128)} %copy-done.5, ...), custom_call_target="tpu_custom_call" | custom-call | tf_op jit(solution)/shard_map/finish/pallas_call | solution.py:1811
  (4 shorter events, 0.0 us)
Async XLA Ops:
  1.5 7.2 %copy-start.5 = (s32[4,16]{1,0:T(4,128)}, s32[4,16]{1,0:T(4,128)S(1)}, u32[]{:S(2)}) copy-start(s32[4,16]{1,0:T(4,128)S(1)} %pad_add_fusion.1.place) | copy-start | bytes 772
  4.7 1.4 copy-start.1
  6.1 1.4 copy-start.2
  8.7 1.1 copy-start
  9.8 0.7 copy-start.3
  10.5 1.1 copy-start.4
  11.6 0.6 copy-start.6
